TPU v7x, 256 devices: a whole 4x4x8 slice. The times are simulated.
256 devices in a mesh: dp: 8 (over x, core), res: 32 (over z, y).
Axes of the slice: x: 4, y: 4, z: 8, core: 2. Of those that a mesh axis runs over, the one named last changes fastest.
Arguments:
- alignment: bfloat16 [8, 128, 256, 256], P('dp', None, 'res'), may hold values from -6 to 6
- chain_ids: int32 [8, 256], P('dp'), may hold values from 0 to 11, never falling along the last dimension, each value on 1 to 64 neighbouring positions
- row_counts: int32 [8, 12], P('dp'), may hold values from 1 to 16, 64 in all within a row
- norm_gain: float32 [256], replicated, may hold values from 0.5 to 1.5
- norm_shift: float32 [256], replicated, may hold values from -3 to 3
- left_weight: bfloat16 [256, 32], replicated, may hold values from -0.375 to 0.375
- left_bias: float32 [32], replicated, may hold values from -3 to 3
- right_weight: bfloat16 [256, 32], replicated, may hold values from -0.375 to 0.375
- right_bias: float32 [32], replicated, may hold values from -3 to 3
- out_weight: bfloat16 [1024, 128], replicated, may hold values from -1 to 1
- out_bias: float32 [128], replicated, may hold values from -3 to 3
- pair_cotangent: bfloat16 [8, 256, 256, 128], P('dp', 'res'), may hold values from -6 to 6
Outputs:
- pair_update: bfloat16 [8, 256, 256, 128], P('dp', 'res')
- alignment_grad: bfloat16 [8, 128, 256, 256], P('dp', None, 'res')
- left_weight_grad: float32 [256, 32], replicated
- left_bias_grad: float32 [32], replicated
- right_weight_grad: float32 [256, 32], replicated
- right_bias_grad: float32 [32], replicated
- out_weight_grad: float32 [1024, 128], replicated
- out_bias_grad: float32 [128], replicated
- norm_gain_grad: float32 [256], replicated
- norm_shift_grad: float32 [256], replicated
Inputs may be any that keep to these rules, and one draw needn't show every extreme that they name: `chain_ids`: never falls along the residues; every chain 0 to 11 holds at least one residue. `row_counts`: each complex's counts sum to 64, and the largest count is exactly 16.
All inputs are finite; a program needn't handle non-finite values.
Results may differ from a plain program's by a relative error of at most 0.018.
Values may be sent and summed in bfloat16 or wider, within the bound.
A program may use at most 128 MiB of HBM per device.

v0:
```python
import math

import jax
import jax.numpy as jnp
from jax import lax
from jax.sharding import PartitionSpec as P

C_M = 256
C_H = 32
C_Z = 128
PAIRED = 64
UNP = 64


EPSILON = 1e-05
NORM_FLOOR = 0.001


def per_residue(lookup, residue_ids):
    labels = jnp.arange(lookup.shape[0], dtype=jnp.int32)
    picked = jnp.where(
        residue_ids[:, None] == labels[None, :], lookup[None, :], jnp.zeros_like(lookup[None, :])
    )
    return jnp.sum(picked, axis=1)


def unpaired_chain(chain_counts):
    row_ends = jnp.cumsum(chain_counts)
    row_place = jnp.arange(UNP, dtype=jnp.int32)
    return jnp.sum((row_place[:, None] >= row_ends[None, :]).astype(jnp.int32), axis=1)


def layer_norm(values, norm_gain, norm_shift):
    floats = values.astype(jnp.float32)
    centred = floats - jnp.mean(floats, axis=-1, keepdims=True)
    inverse = lax.rsqrt(jnp.mean(centred * centred, axis=-1, keepdims=True) + EPSILON)
    scaled = centred * inverse
    normed = (scaled * norm_gain + norm_shift).astype(jnp.bfloat16)
    return (scaled, inverse, normed)


def project(normed, weight, offset, row_mask):
    channels = normed.shape[-1]
    flattened = normed.reshape(-1, channels)
    result = jnp.dot(flattened, weight, preferred_element_type=jnp.float32) + offset
    result = result.reshape(normed.shape[:-1] + (weight.shape[1],))
    return (result * row_mask[..., None]).astype(jnp.bfloat16)


def norm_backward(grad_normed, scaled, inverse, norm_gain):
    grad_scaled = grad_normed * norm_gain
    mean_grad = jnp.mean(grad_scaled, axis=-1, keepdims=True)
    mean_prod = jnp.mean(grad_scaled * scaled, axis=-1, keepdims=True)
    return inverse * (grad_scaled - mean_grad - scaled * mean_prod)


def outer_block(left_part, right_part):
    count = left_part.shape[0]
    rows_i = left_part.shape[1]
    cols_j = right_part.shape[1]
    products = lax.dot_general(
        left_part.reshape(count, rows_i * C_H),
        right_part.reshape(count, cols_j * C_H),
        (((0,), (0,)), ((), ())),
        preferred_element_type=jnp.float32,
    )
    return jnp.transpose(products.reshape(rows_i, C_H, cols_j, C_H), (0, 2, 1, 3))


def body(
    alignment,
    chain_ids,
    row_counts,
    norm_gain,
    norm_shift,
    left_weight,
    left_bias,
    right_weight,
    right_bias,
    out_weight,
    out_bias,
    pair_cotangent,
):
    local_rows = alignment[0]
    pair_local = pair_cotangent[0]
    rows_dev = local_rows.shape[1]
    residues = chain_ids.shape[1]
    all_chains = chain_ids[0]
    chain_counts = row_counts[0]
    own_start = lax.axis_index("res") * rows_dev
    own_chains = lax.dynamic_slice_in_dim(all_chains, own_start, rows_dev, 0)
    row_chain = unpaired_chain(chain_counts)
    unpaired_mask = (row_chain[:, None] == own_chains[None, :]).astype(jnp.float32)
    own_mask = jnp.concatenate([jnp.ones((PAIRED, rows_dev), jnp.float32), unpaired_mask], axis=0)
    same_own = (own_chains[:, None] == all_chains[None, :]).astype(jnp.float32)
    own_counts = per_residue(chain_counts, own_chains).astype(jnp.float32)
    normalizer = PAIRED + same_own * own_counts[:, None] + NORM_FLOOR
    scaled, inverse, normed = layer_norm(local_rows, norm_gain, norm_shift)
    left_rows = project(normed, left_weight, left_bias, own_mask)
    right_rows = project(normed, right_weight, right_bias, own_mask)
    own_factor = jnp.ones_like(same_own)
    right_all = lax.all_gather(right_rows, "res", axis=1, tiled=True)
    kept = left_rows.shape[0]
    left_paired = left_rows[:PAIRED]
    left_unpaired = left_rows[PAIRED:]
    col_block = math.gcd(residues, 128)

    def column_step(totals, block_index):
        weight_total, paired_grad, unpaired_grad = totals
        col_start = block_index * col_block
        right_block = lax.dynamic_slice_in_dim(right_all, col_start, col_block, 1)
        factor_block = lax.dynamic_slice_in_dim(own_factor, col_start, col_block, 1)
        norm_block = lax.dynamic_slice_in_dim(normalizer, col_start, col_block, 1)[:, :, None, None]
        grad_block = lax.dynamic_slice_in_dim(pair_local, col_start, col_block, 1).reshape(
            rows_dev * col_block, C_Z
        )
        paired_prod = outer_block(left_paired, right_block[:PAIRED])
        unpaired_prod = outer_block(left_unpaired, right_block[PAIRED:])
        products = paired_prod + unpaired_prod * factor_block[:, :, None, None]
        outer_mean = (
            (products / norm_block).astype(jnp.bfloat16).reshape(rows_dev * col_block, C_H * C_H)
        )
        update = (
            jnp.dot(outer_mean, out_weight, preferred_element_type=jnp.float32) + out_bias
        ).astype(jnp.bfloat16)
        weight_total = weight_total + lax.dot_general(
            outer_mean, grad_block, (((0,), (0,)), ((), ())), preferred_element_type=jnp.float32
        )
        back = lax.dot_general(
            grad_block, out_weight, (((1,), (1,)), ((), ())), preferred_element_type=jnp.float32
        )
        outer_grad = (back.reshape(rows_dev, col_block, C_H, C_H) / norm_block).astype(jnp.bfloat16)
        masked_grad = outer_grad * factor_block.astype(jnp.bfloat16)[:, :, None, None]
        paired_grad = paired_grad + jnp.einsum(
            "ijce,sje->sic", outer_grad, right_block[:PAIRED], preferred_element_type=jnp.float32
        )
        unpaired_grad = unpaired_grad + jnp.einsum(
            "ijce,sje->sic", masked_grad, right_block[PAIRED:], preferred_element_type=jnp.float32
        )
        new_totals = (weight_total, paired_grad, unpaired_grad)
        column_terms = jnp.concatenate(
            [
                jnp.einsum(
                    "ijce,sic->jse", outer_grad, left_paired, preferred_element_type=jnp.float32
                ),
                jnp.einsum(
                    "ijce,sic->jse", masked_grad, left_unpaired, preferred_element_type=jnp.float32
                ),
            ],
            axis=1,
        )
        return (new_totals, (update.reshape(rows_dev, col_block, C_Z), column_terms))

    start_totals = (
        jnp.zeros((C_H * C_H, C_Z), jnp.float32),
        jnp.zeros((PAIRED, rows_dev, C_H), jnp.float32),
        jnp.zeros((kept - PAIRED, rows_dev, C_H), jnp.float32),
    )
    block_ids = jnp.arange(residues // col_block, dtype=jnp.int32)
    totals, outputs = lax.scan(column_step, start_totals, block_ids)
    out_weight_grad, paired_grad, unpaired_grad = totals
    updates, column_terms = outputs
    pair_update = jnp.transpose(updates, (1, 0, 2, 3)).reshape(rows_dev, residues, C_Z)
    left_grad = jnp.concatenate([paired_grad, unpaired_grad], axis=0)
    own_columns = lax.psum_scatter(
        column_terms.reshape(residues, kept, C_H).astype(jnp.bfloat16),
        "res",
        scatter_dimension=0,
        tiled=True,
    ).astype(jnp.float32)
    right_grad = jnp.transpose(own_columns, (1, 0, 2))
    left_act = (left_grad * own_mask[..., None]).astype(jnp.bfloat16)
    right_act = (right_grad * own_mask[..., None]).astype(jnp.bfloat16)
    flat_normed = normed.reshape(-1, C_M)
    flat_left = left_act.reshape(-1, C_H)
    flat_right = right_act.reshape(-1, C_H)
    contract_rows = (((0,), (0,)), ((), ()))
    left_weight_grad = lax.dot_general(
        flat_normed, flat_left, contract_rows, preferred_element_type=jnp.float32
    )
    right_weight_grad = lax.dot_general(
        flat_normed, flat_right, contract_rows, preferred_element_type=jnp.float32
    )
    left_bias_grad = jnp.sum(flat_left.astype(jnp.float32), axis=0)
    right_bias_grad = jnp.sum(flat_right.astype(jnp.float32), axis=0)
    contract_cols = (((1,), (1,)), ((), ()))
    grad_normed = lax.dot_general(
        flat_left, left_weight, contract_cols, preferred_element_type=jnp.float32
    )
    grad_normed = grad_normed + lax.dot_general(
        flat_right, right_weight, contract_cols, preferred_element_type=jnp.float32
    )
    grad_normed = grad_normed.reshape(local_rows.shape[0], rows_dev, C_M)
    gain_grad = jnp.sum(grad_normed * scaled, axis=(0, 1))
    shift_grad = jnp.sum(grad_normed, axis=(0, 1))
    alignment_grad = norm_backward(grad_normed, scaled, inverse, norm_gain).astype(jnp.bfloat16)
    out_bias_grad = jnp.sum(pair_local.astype(jnp.float32), axis=(0, 1))
    summed = lax.psum(
        (
            left_weight_grad,
            left_bias_grad,
            right_weight_grad,
            right_bias_grad,
            out_weight_grad,
            out_bias_grad,
            gain_grad,
            shift_grad,
        ),
        ("dp", "res"),
    )
    scaled_sums = [entry / residues for entry in summed]
    return (
        pair_update[None],
        alignment_grad[None],
        scaled_sums[0],
        scaled_sums[1],
        scaled_sums[2],
        scaled_sums[3],
        scaled_sums[4],
        scaled_sums[5],
        scaled_sums[6],
        scaled_sums[7],
    )


def solution(mesh):
    return jax.shard_map(
        body,
        mesh=mesh,
        in_specs=(
            P("dp", None, "res", None),
            P("dp", None),
            P("dp", None),
            P(),
            P(),
            P(),
            P(),
            P(),
            P(),
            P(),
            P(),
            P("dp", "res", None, None),
        ),
        out_specs=(
            P("dp", "res", None, None),
            P("dp", None, "res", None),
            P(),
            P(),
            P(),
            P(),
            P(),
            P(),
            P(),
            P(),
        ),
        check_vma=False,
    )
```

profile of v0, /device:TPU:1, one launch (start us, length us, event | category | flops | bytes accessed | tf_op | source)
XLA Modules:
  0.0 951.4 jit_solution(4957662144740580138)
XLA Ops:
  18.2 76.9 %all-gather.2.cloned.1.call-done = bf16[128,256,32]{0,2,1:T(8,128)(2,1)} async-done(((bf16[128,8,32]{0,2,1:T(8,128)(2,1)}), bf16[128,256,32]{0,2,1:T(8,128)(2,1)}) %all-gather.2.cloned.1.call-update) | async-done | bytes 2097168 | tf_op jit(solution)/shard_map/all_gather | solution.py:102
  95.6 120.9 %while.19 = (s32[]{:T(128)}, f32[1024,128]{1,0:T(8,128)}, f32[64,8,32]{0,2,1:T(8,128)}, f32[64,8,32]{0,2,1:T(8,128)}, bf16[2,8,128,128]{3,2,1,0:T(8,128)(2,1)}, ...) while((s32[]{:T(128)}, f32[1024,128]{1,0:T(8,128)}, ...), condition=%wide.region_6.7_spmd.clone, body=%wide.region_5.6_spmd.clone.sunk | while | flops 1618542592 | bytes 76712896 | solution.py:160
  99.8 2.0 constant_dynamic-slice_fusion.8
  104.0 1.7 divide_convert_fusion.3
  107.2 1.6 fusion.145
  110.5 1.7 copy.206
  112.2 2.3 constant_dynamic-update-slice_fusion.5
  115.2 2.7 fusion.142
  117.9 5.6 copy.202
  123.5 10.8 %add.186 = f32[8,32,128,32]{3,2,1,0:T(8,128)} reshape(f32[256,4096]{1,0:T(8,128)} %copy.202) | data formatting | bytes 8388608 | tf_op jit(solution)/shard_map/while/body/eval_jaxpr/add | solution.py:119
  134.2 9.7 %fusion.143 = bf16[8,128,32,32]{3,1,2,0:T(8,128)(2,1)} fusion(f32[8,32,128,32]{3,2,1,0:T(8,128)} %add.186, f32[8,128]{1,0:T(8,128)S(1)} %copy-done.12), kind=kLoop, calls=%fused_computation.1.clone.1 | loop fusion | flops 2097152 | bytes 6295552 | tf_op jit(solution)/shard_map/while/body/eval_jaxpr/convert_element_type | solution.py:121
  143.9 6.9 copy.203
  150.9 1.5 fusion.144
  152.4 1.8 fusion.147
  159.2 2.0 constant_dynamic-slice_fusion.8
  163.5 1.7 divide_convert_fusion.3
  166.7 2.5 fusion.145
  170.9 1.7 copy.206
  172.6 2.3 constant_dynamic-update-slice_fusion.5
  175.6 2.7 fusion.142
  178.3 5.6 copy.202
  183.9 10.8 %add.186 = f32[8,32,128,32]{3,2,1,0:T(8,128)} reshape(f32[256,4096]{1,0:T(8,128)} %copy.202) | data formatting | bytes 8388608 | tf_op jit(solution)/shard_map/while/body/eval_jaxpr/add | solution.py:119
  194.6 9.7 %fusion.143 = bf16[8,128,32,32]{3,1,2,0:T(8,128)(2,1)} fusion(f32[8,32,128,32]{3,2,1,0:T(8,128)} %add.186, f32[8,128]{1,0:T(8,128)S(1)} %copy-done.12), kind=kLoop, calls=%fused_computation.1.clone.1 | loop fusion | flops 2097152 | bytes 6295552 | tf_op jit(solution)/shard_map/while/body/eval_jaxpr/convert_element_type | solution.py:121
  204.3 6.9 copy.203
  211.3 2.6 fusion.144
  213.9 1.8 fusion.147
  217.6 1.8 convert_reduce_fusion.1
  220.3 248.0 %all-reduce.5.cloned.1.call-done = f32[1024,128]{1,0:T(8,128)} async-done(((f32[1024,128]{1,0:T(8,128)}), f32[1024,128]{1,0:T(8,128)}) %all-reduce.5.cloned.1.call-update) | async-done | bytes 524304 | tf_op jit(solution)/shard_map/psum | solution.py:198
  468.3 1.9 broadcast_multiply_fusion
  470.2 213.2 %reduce-scatter.2.cloned.1.call-done = bf16[8,128,32]{1,2,0:T(8,128)(2,1)} async-done(((bf16[256,128,32]{1,2,0:T(8,128)(2,1)}), bf16[8,128,32]{1,2,0:T(8,128)(2,1)}) %reduce-scatter.2.cloned.1.call-update) | async-done | bytes 65552 | tf_op jit(solution)/shard_map/reduce_scatter | solution.py:165
  683.4 1.7 convert_reduce_fusion.2
  691.3 248.7 %all-reduce.7.cloned.1.call-done = (f32[256,32]{0,1:T(8,128)}, f32[32]{0:T(128)}, f32[256,32]{0,1:T(8,128)}, f32[32]{0:T(128)}, f32[128]{0:T(128)}, /*index=5*/f32[256]{0:T(256)}, f32[256]{0:T(256)}) async-done(((f32[256,32]{0,1:T(8,128)}, f32[32]{0:T(128)}, f32[256,32]{0,1:T(8,128)}, f32[32]{0:T(128)}, f32[128]{0:T(128)}, /*index=5*/f32[256]{0:T(256)}, f32[256]{0:T(256)}), (f32[256,32]{0,1:T(8,128)}, ...) | async-done | bytes 68368 | tf_op jit(solution)/shard_map/psum | solution.py:198
  (151 shorter events, 45.0 us)
Async XLA Ops:
  7.2 7.8 copy-start
  7.2 6.8 copy-start.1
  7.2 7.8 copy-start.27
  7.2 87.9 %all-gather.2.cloned.1.call-start = ((), (), s32[]{:S(2)}) async-start(), calls=%async_computation.1 | async-start | bytes 2162688 | tf_op jit(solution)/shard_map/all_gather | solution.py:102
  8.6 4.0 copy-start.3
  8.6 7.1 copy-start.16
  8.6 7.1 copy-start.28
  8.7 4.6 copy-start.20
  12.6 3.8 copy-start.18
  15.0 2.2 copy-start.29
  15.0 2.4 copy-start.25
  17.1 451.2 %all-reduce.5.cloned.1.call-start = ((), (), s32[]{:S(2)}) async-start(), calls=%async_computation.3 | async-start | bytes 1048576 | tf_op jit(solution)/shard_map/psum | solution.py:198
  104.0 1.7 copy-start.13
  123.5 10.8 %copy-start.12 = (f32[8,128]{1,0:T(8,128)S(1)}, f32[8,128]{1,0:T(8,128)}, u32[]{:S(2)}) copy-start(f32[8,128]{1,0:T(8,128)} %constant_dynamic-slice_fusion.9) | copy-start | bytes 12292 | tf_op jit(solution)/shard_map/while
  152.4 1.8 copy-start.9
  163.5 1.7 copy-start.13
  183.9 10.8 %copy-start.12 = (f32[8,128]{1,0:T(8,128)S(1)}, f32[8,128]{1,0:T(8,128)}, u32[]{:S(2)}) copy-start(f32[8,128]{1,0:T(8,128)} %constant_dynamic-slice_fusion.9) | copy-start | bytes 12292 | tf_op jit(solution)/shard_map/while
  211.3 2.6 copy-start.30
  213.9 1.8 copy-start.9
  216.5 3.0 copy-start.11
  216.5 466.9 %reduce-scatter.2.cloned.1.call-start = ((), (), s32[]{:S(2)}) async-start(), calls=%async_computation.2 | async-start | bytes 2162688 | tf_op jit(solution)/shard_map/reduce_scatter | solution.py:165
  216.6 466.8 %copy-start.15 = (f32[64,8,32]{0,2,1:T(8,128)S(1)}, f32[64,8,32]{0,2,1:T(8,128)}, u32[]{:S(2)}) copy-start(f32[64,8,32]{0,2,1:T(8,128)} %get-tuple-element.88) | copy-start | bytes 196612
  216.6 466.8 %copy-start.19 = (f32[128,8]{0,1:T(8,128)S(1)}, f32[128,8]{0,1:T(8,128)}, u32[]{:S(2)}) copy-start(f32[128,8]{0,1:T(8,128)} %copy-done.18) | copy-start | bytes 12292
  217.3 468.0 %copy-start.2 = (bf16[1,128,8,256]{3,2,1,0:T(8,128)(2,1)S(1)}, bf16[1,128,8,256]{3,2,1,0:T(8,128)(2,1)}, u32[]{:S(2)}) copy-start(bf16[1,128,8,256]{3,2,1,0:T(8,128)(2,1)} %param.14) | copy-start | bytes 1572868
  217.3 468.0 %copy-start.4 = (f32[128,8]{1,0:T(8,128)S(1)}, f32[128,8]{1,0:T(8,128)}, u32[]{:S(2)}) copy-start(f32[128,8]{1,0:T(8,128)} %copy-done.3) | copy-start | bytes 12292
  217.3 468.0 %copy-start.6 = (f32[128,8]{1,0:T(8,128)S(1)}, f32[128,8]{1,0:T(8,128)}, u32[]{:S(2)}) copy-start(f32[128,8]{1,0:T(8,128)} %copy-done.5) | copy-start | bytes 12292
  217.3 468.0 %copy-start.24 = (f32[256]{0:T(256)S(1)}, f32[256]{0:T(256)}, u32[]{:S(2)}) copy-start(f32[256]{0:T(256)} %param.17) | copy-start | bytes 3076
  217.3 468.0 %copy-start.26 = (f32[256]{0:T(256)S(1)}, f32[256]{0:T(256)}, u32[]{:S(2)}) copy-start(f32[256]{0:T(256)} %param.18) | copy-start | bytes 3076
  217.3 722.6 %all-reduce.7.cloned.1.call-start = ((), (), s32[]{:S(2)}) async-start(), calls=%async_computation.4 | async-start | bytes 138240 | tf_op jit(solution)/shard_map/psum | solution.py:198
  686.5 1.6 copy-start.17
  686.7 1.8 copy-start.21
  686.7 1.8 copy-start.23
  (9 other events, 7.4 us)
Sparse Core Ops, SparseCore 0:
  17.2 77.8 all-gather.1
  216.6 251.6 all-reduce.4
  472.2 211.1 reduce-scatter.1
  692.0 247.9 all-reduce.6
where the time goes:
time: 953 us; the launch traced here: 951 us
  waiting for transfers between devices  788 us (83%)
  local copies, waits for them, and re-layouts  79.1 us (8%)
  other arithmetic  37.6 us (4%)
  matrix products  31.1 us (3%)
  between operations  14.2 us (1%)
    psum x2, waiting for transfers between devices, body(): lax.psum((left_weight_grad, left_bias_grad, right_weight_grad, right_bias...  497 us
    reduce_scatter x1, waiting for transfers between devices, body(): lax.psum_scatter(column_terms.reshape(residues, kept, C_H).astype(jnp.bfl...  213 us
    all_gather x1, waiting for transfers between devices, body(): right_all = lax.all_gather(right_rows, 'res', axis=1, tiled=True)  76.9 us
    add x4, local copies, waits for them, and re-layouts, column_step(): products = paired_prod + unpaired_prod * factor_block[:, :, None, None]  32.7 us
    convert_element_type x2, other arithmetic, column_step(): (products / norm_block).astype(jnp.bfloat16)  19.4 us
  transfers between devices with their start and end apart: 4, of which 4 were waited for; matrix products, arithmetic and copies ran while one was open for 1% of the time, Pallas kernels for 0%

commit v1 on v0

v1 whole, which is shorter than its diff:
```python
import functools

import jax
import jax.numpy as jnp
from jax import lax
from jax.experimental import pallas as pl
from jax.experimental.pallas import tpu as pltpu
from jax.sharding import PartitionSpec as P

C_M = 256
C_H = 32
C_Z = 128
PAIRED = 64
UNP = 64
MOST = 16
CHAINS = 12
EPSILON = 1e-05
NORM_FLOOR = 0.001

ROWS = 8
SLOTS = PAIRED + MOST
NY, NZ, NDP = 4, 8, 8
NRES = NY * NZ
N = ROWS * NRES
ENT = ROWS * SLOTS
F32, BF16 = jnp.float32, jnp.bfloat16
MESH = pl.DeviceIdType.MESH

NN = (((1,), (0,)), ((), ()))
NT = (((1,), (1,)), ((), ()))
TN = (((0,), (0,)), ((), ()))


def dot(a, b, dims=NN):
    return lax.dot_general(a, b, dims, preferred_element_type=F32)


def iota(shape, dim):
    return lax.broadcasted_iota(jnp.int32, shape, dim)


def onehot(cond):
    return jnp.where(cond, 1.0, 0.0).astype(BF16)


def kernel(
    chain_s, counts_s, chain_v, x_ref, gain_ref, shift_ref, wt_ref, bias_ref, biascol_ref,
    w2_ref, obias_ref, cot_ref,
    upd_ref, agrad_ref, dw_ref, small_ref,
    xc, normed, inv_ref, lrow, lt, q_ref, tp, tu, g_ref, gm_ref, v_ref, rx, rp, ru,
    ry, vsum, rz, ucat, dwf, dws, a_rx, s1, b_rx, c_rx, s3, s4, d_rx,
    sm, t_rx, sm1, e_rx, sm2, f_rx, sm3, sm_out, ract,
    agz_s, agz_r, agy_s, agy_r, rsy_s, rsy_r, rsz_s, rsz_r,
    p_s, p_r, bz_s, bz_r, cy_s, cy_r, dz_s, dz_r, ed_s, ed_r,
    tz_s, tz_r, ud_s, ud_r, uy_s, uy_r, uz_s, uz_r,
):
    me = lax.axis_index("res")
    dp = lax.axis_index("dp")
    z, y = me // NY, me % NY

    def zpeer(k):
        return (z + k) % NZ

    def ypeer(k):
        return (y + k) % NY

    def dpeer(k):
        return (dp + k) % NDP

    def rc(src, dst, ss, rs, **where):
        return pltpu.make_async_remote_copy(
            src_ref=src, dst_ref=dst, send_sem=ss, recv_sem=rs,
            device_id=where, device_id_type=MESH,
        )

    barrier = pltpu.get_barrier_semaphore()
    for k in range(1, NZ):
        pl.semaphore_signal(barrier, inc=1, device_id={"res": zpeer(k) * NY + y}, device_id_type=MESH)
    for k in range(1, NY):
        pl.semaphore_signal(barrier, inc=1, device_id={"res": z * NY + ypeer(k)}, device_id_type=MESH)
    for k in range(1, NDP):
        pl.semaphore_signal(barrier, inc=1, device_id={"dp": dpeer(k)}, device_id_type=MESH)

    chain, start, count, base = [], [], [], []
    for r in range(ROWS):
        c = chain_s[0, me * ROWS + r]
        st = jnp.int32(0)
        ct = jnp.int32(0)
        for k in range(CHAINS):
            v = counts_s[0, k]
            st = st + jnp.where(c > k, v, 0)
            ct = ct + jnp.where(c == k, v, 0)
        chain.append(c)
        start.append(st)
        count.append(ct)
        base.append(jnp.minimum(st, UNP - MOST))

    def slot_mask(r, shape, dim):
        s = iota(shape, dim)
        row = s - PAIRED + base[r]
        live = (row >= start[r]) & (row < start[r] + count[r])
        return jnp.where((s < PAIRED) | live, 1.0, 0.0)

    ro, co = iota((128, 128), 0), iota((128, 128), 1)
    perm0 = onehot(co == (ro % 16) * ROWS + ro // 16)
    for b in range(PAIRED // 16):
        part = dot(perm0, x_ref[b * 128:(b + 1) * 128, :])
        for r in range(ROWS):
            xc[r * SLOTS + b * 16:r * SLOTS + b * 16 + 16, :] = part[r * 16:(r + 1) * 16]
    ru_i = iota((128, UNP * ROWS), 0)
    base_rows = jnp.zeros((128, UNP * ROWS), jnp.int32)
    for r in range(ROWS):
        base_rows = jnp.where(ru_i // 16 == r, base[r], base_rows)
    pick = onehot(iota((128, UNP * ROWS), 1) == (base_rows + ru_i % 16) * ROWS + ru_i // 16)
    part = dot(pick, x_ref[PAIRED * ROWS:, :])
    for r in range(ROWS):
        xc[r * SLOTS + PAIRED:(r + 1) * SLOTS, :] = part[r * 16:(r + 1) * 16]

    for r in range(ROWS):
        rows = slice(r * SLOTS, (r + 1) * SLOTS)
        floats = xc[rows, :]
        centred = floats - jnp.mean(floats, axis=-1, keepdims=True)
        inverse = lax.rsqrt(jnp.mean(centred * centred, axis=-1, keepdims=True) + EPSILON)
        scaled = centred * inverse
        nrm = (scaled * gain_ref[...] + shift_ref[...]).astype(BF16)
        xc[rows, :] = scaled
        inv_ref[rows, :] = inverse
        normed[rows, :] = nrm
        left = (dot(nrm, wt_ref[0:C_H, :], NT) + bias_ref[0:1, :]) * slot_mask(r, (SLOTS, C_H), 0)
        lrow[rows, :] = left.astype(BF16)
        right = (dot(wt_ref[C_H:, :], nrm, NT) + biascol_ref[C_H:, :]) * slot_mask(r, (C_H, SLOTS), 1)
        q_ref[r * C_H:(r + 1) * C_H, 0:SLOTS] = right.astype(BF16)
    re, ce = iota((256, 256), 0), iota((256, 256), 1)
    permq = onehot(ce == (re % 8) * 32 + ((re // 8) % 2) * 16 + re // 16)
    mixed = dot(permq, q_ref[:, 0:SLOTS])
    for p in range(8):
        rx[me, :, p * 128:(p + 1) * 128] = jnp.concatenate(
            [mixed[(2 * p + a) * 16:(2 * p + a + 1) * 16, 0:PAIRED] for a in range(2)], axis=1
        ).astype(BF16)
    for q in range(2):
        rx[me, :, 1024 + q * 128:1024 + (q + 1) * 128] = jnp.concatenate(
            [mixed[(8 * q + a) * 16:(8 * q + a + 1) * 16, PAIRED:SLOTS] for a in range(8)], axis=1
        ).astype(BF16)

    pl.semaphore_wait(barrier, NZ + NY + NDP - 3)

    def agz(k):
        return rc(rx.at[me], rx.at[me], agz_s.at[k], agz_r.at[k], res=zpeer(k) * NY + y)

    for k in (1, 7, 2, 6, 3, 5, 4):
        agz(k).start()

    lt[...] = jnp.transpose(lrow[...].astype(F32)).astype(BF16)

    @pl.loop(0, 16)
    def _(g):
        h, p = g // 8, g % 8
        t = dot(lrow[...], w2_ref[:, pl.ds(pl.multiple_of(g * 256, 256), 256)]).astype(BF16)
        rowp = pl.multiple_of((p * 2 + h) * 128, 128)
        rowu = pl.multiple_of(((p // 4) * 2 + h) * 128 + (p % 4) * 32, 32)
        for i in range(ROWS):
            for a in range(2):
                tp[pl.ds(rowp + a * 64, 64), i * 128:(i + 1) * 128] = t[i * SLOTS:i * SLOTS + PAIRED, a * 128:(a + 1) * 128]
                tu[pl.ds(rowu + a * 16, 16), i * 128:(i + 1) * 128] = t[i * SLOTS + PAIRED:(i + 1) * SLOTS, a * 128:(a + 1) * 128]

    def agy(k, kz):
        slot = ((z - kz + NZ) % NZ) * NY + y
        return rc(rx.at[slot], rx.at[slot], agy_s.at[k, kz], agy_r.at[k, kz], res=z * NY + ypeer(k))

    for kz in (0, 1, 7, 2, 6, 3, 5, 4):
        if kz:
            agz(kz).wait_recv()
        for k in (1, 3, 2):
            agy(k, kz).start()

    chain_col = jnp.transpose(jnp.broadcast_to(chain_v[...].astype(F32), (128, N)))
    obg = jnp.zeros((8, C_Z), F32)
    inv_own = []
    for i in range(ROWS):
        same = chain_col == chain[i].astype(F32)
        cntf = jnp.full((8, C_Z), count[i].astype(F32))
        inv_own.append((1.0 / (PAIRED + cntf + NORM_FLOOR))[0:1, :])
        raw = cot_ref[i].astype(F32)
        obg = obg + jnp.sum(raw.reshape(N // 8, 8, C_Z), axis=0)
        g = (raw * jnp.where(same, inv_own[i], 1.0 / (PAIRED + NORM_FLOOR))).astype(BF16)
        g_ref[:, i * 128:(i + 1) * 128] = g
        gm_ref[:, i * 128:(i + 1) * 128] = jnp.where(same, g.astype(F32), 0.0).astype(BF16)

    def put_v(v, lane):
        both = jnp.concatenate(
            [v[:, 0:128].reshape(NRES, ROWS, 128), v[:, 128:256].reshape(NRES, ROWS, 128)], axis=1
        )
        v_ref[:, :, pl.ds(lane, 128)] = both.astype(BF16)

    @pl.loop(0, 8)
    def _(p):
        put_v(dot(g_ref[...], tp[pl.ds(pl.multiple_of(p * 256, 256), 256), :], NT), pl.multiple_of(p * 128, 128))

    for q in range(2):
        put_v(dot(gm_ref[...], tu[q * 256:(q + 1) * 256, :], NT), 1024 + q * 128)

    def rsy(k, kz):
        dst = zpeer(kz) * NY + ypeer(k)
        return rc(v_ref.at[dst], ry.at[k, kz], rsy_s.at[k, kz], rsy_r.at[k, kz], res=z * NY + ypeer(k))

    for kz in (1, 7, 2, 6, 3, 5, 4, 0):
        for k in (1, 3, 2):
            rsy(k, kz).start()

    for kz in range(NZ):
        for k in range(1, NY):
            agy(k, kz).wait_recv()

    @pl.loop(0, NRES // 2)
    def _(d):
        a, b = rx[2 * d].astype(F32), rx[2 * d + 1].astype(F32)
        rows = pl.ds(pl.multiple_of(d * 16, 16), 16)
        for h in range(2):
            both = jnp.concatenate([a[h * 8:h * 8 + 8], b[h * 8:h * 8 + 8]], axis=0).astype(BF16)
            for p in range(8):
                rp[rows, p * 256 + h * 128:p * 256 + (h + 1) * 128] = both[:, p * 128:(p + 1) * 128]
            for q in range(2):
                ru[rows, q * 256 + h * 128:q * 256 + (h + 1) * 128] = both[:, 1024 + q * 128:1024 + (q + 1) * 128]

    @pl.loop(0, 8)
    def _(p):
        u = dot(rp[:, pl.ds(pl.multiple_of(p * 256, 256), 256)], g_ref[...], TN).astype(BF16)
        for h in range(2):
            for a in range(2):
                lane = pl.multiple_of((h * 16 + 2 * p + a) * 128, 128)
                for i in range(ROWS):
                    ucat[i * SLOTS:i * SLOTS + PAIRED, pl.ds(lane, 128)] = u[(h * 2 + a) * 64:(h * 2 + a + 1) * 64, i * 128:(i + 1) * 128]

    for q in range(2):
        u = dot(ru[:, q * 256:(q + 1) * 256], gm_ref[...], TN).astype(BF16)
        for h in range(2):
            for a in range(8):
                lane = (h * 16 + q * 8 + a) * 128
                for i in range(ROWS):
                    ucat[i * SLOTS + PAIRED:(i + 1) * SLOTS, lane:lane + 128] = u[(h * 8 + a) * 16:(h * 8 + a + 1) * 16, i * 128:(i + 1) * 128]

    @pl.loop(0, 16)
    def _(g):
        dw = dot(lt[...], ucat[:, pl.ds(pl.multiple_of(g * 256, 256), 256)])
        for a in range(2):
            part = dw[:, a * 128:(a + 1) * 128]
            row = pl.multiple_of((g % 2) * 64 + a * 32, 32)
            dwf[g // 2, pl.ds(row, 32), :] = part
            dws[g // 2, pl.ds(row, 32), :] = part.astype(BF16)

    def pdp(k):
        return rc(dws.at[dpeer(k)], a_rx.at[k], p_s.at[k], p_r.at[k], dp=dpeer(k))

    for k in range(1, NDP):
        pdp(k).start()

    def rsz(k):
        return rc(vsum.at[k], rz.at[k], rsz_s.at[k], rsz_r.at[k], res=zpeer(k) * NY + y)

    own = None
    for kz in (1, 7, 2, 6, 3, 5, 4, 0):
        total = v_ref[zpeer(kz) * NY + y].astype(F32)
        for k in range(1, NY):
            rsy(k, kz).wait_recv()
            total = total + ry[k, kz].astype(F32)
        if kz:
            vsum[kz] = total.astype(BF16)
            rsz(kz).start()
        else:
            own = total

    def left_step(k, acc):
        cols = pl.ds(pl.multiple_of(k * 512, 512), 512)
        return acc + dot(ucat[:, cols], w2_ref[:, cols], NT)

    lgrad = lax.fori_loop(0, 8, left_step, jnp.zeros((ENT, C_H), F32))

    @pl.loop(0, 4)
    def _(g):
        cols = pl.ds(pl.multiple_of(g * 256, 256), 256)
        main = dot(rp[...], tp[:, cols])
        side = dot(ru[...], tu[:, cols])
        for a in range(2):
            i = 2 * g + a
            ch = jnp.int32(0)
            iv = jnp.zeros((1, C_Z), F32)
            for r in range(ROWS):
                ch = jnp.where(i == r, chain[r], ch)
                iv = jnp.where(i == r, inv_own[r], iv)
            same = chain_col == ch.astype(F32)
            m, s = main[:, a * 128:(a + 1) * 128], side[:, a * 128:(a + 1) * 128]
            out = jnp.where(same, (m + s) * iv, m * (1.0 / (PAIRED + NORM_FLOOR))) + obias_ref[...]
            upd_ref[i] = out.astype(BF16)

    s = dwf[dp]
    for k in range(1, NDP):
        pdp(k).wait_recv()
        s = s + a_rx[k].astype(F32)
    s1[...] = s.reshape(NZ, 16, C_Z)

    def bz(k):
        return rc(s1.at[zpeer(k)], b_rx.at[k], bz_s.at[k], bz_r.at[k], res=zpeer(k) * NY + y)

    for k in range(1, NZ):
        bz(k).start()

    for kz in range(1, NZ):
        rsz(kz).wait_recv()
        own = own + rz[kz].astype(F32)
    tiles = []
    for e in range(16):
        tiles.append(jnp.concatenate([own[:, e * 64:(e + 1) * 64], own[:, 1024 + e * 16:1024 + (e + 1) * 16]], axis=1))
    back = dot(permq, jnp.concatenate(tiles, axis=0).astype(BF16), TN)

    gw_l = jnp.zeros((C_H, C_M), F32)
    gw_r = jnp.zeros((C_H, C_M), F32)
    gb_l = jnp.zeros((1, C_H), F32)
    gb_r = jnp.zeros((C_H, 1), F32)
    gain_g = jnp.zeros((1, C_M), F32)
    shift_g = jnp.zeros((1, C_M), F32)
    for r in range(ROWS):
        rows = slice(r * SLOTS, (r + 1) * SLOTS)
        nrm = normed[rows, :]
        lact = (lgrad[rows] * slot_mask(r, (SLOTS, C_H), 0)).astype(BF16)
        ract_t = (back[r * C_H:(r + 1) * C_H, :] * slot_mask(r, (C_H, SLOTS), 1)).astype(BF16)
        gw_l = gw_l + dot(lact, nrm, TN)
        gw_r = gw_r + dot(ract_t, nrm)
        gb_l = gb_l + jnp.sum(lact.astype(F32), axis=0, keepdims=True)
        gb_r = gb_r + jnp.sum(ract_t.astype(F32), axis=1, keepdims=True)
        gn = dot(lact, wt_ref[0:C_H, :]) + dot(ract_t, wt_ref[C_H:, :], TN)
        scaled = xc[rows, :]
        gs = gn * scaled
        gain_g = gain_g + jnp.sum(gs, axis=0, keepdims=True)
        shift_g = shift_g + jnp.sum(gn, axis=0, keepdims=True)
        gg = gn * gain_ref[...]
        mean_g = jnp.mean(gg, axis=-1, keepdims=True)
        mean_p = jnp.mean(gg * scaled, axis=-1, keepdims=True)
        ract[rows, :] = (inv_ref[rows, :] * (gg - mean_g - scaled * mean_p)).astype(BF16)

    smf = jnp.concatenate([gw_l, gw_r], axis=0)
    gbr_row = jnp.transpose(jnp.broadcast_to(gb_r, (C_H, 128)))[0:1, :]
    rows8 = iota((8, C_Z), 0)
    tail = jnp.zeros((8, C_Z), F32)
    tail_rows = (
        gain_g[:, 0:128], gain_g[:, 128:256], shift_g[:, 0:128], shift_g[:, 128:256],
        jnp.sum(obg, axis=0, keepdims=True),
        jnp.concatenate([gb_l, gbr_row, jnp.zeros((1, 64), F32)], axis=1),
    )
    for k, row in enumerate(tail_rows):
        tail = jnp.where(rows8 == k, row, tail)
    flat = jnp.concatenate([smf[:, 0:128], smf[:, 128:256], tail, jnp.zeros((56, C_Z), F32)], axis=0)
    sm[...] = flat.reshape(NZ, 24, C_Z)

    def tz(k):
        return rc(sm.at[zpeer(k)], t_rx.at[k], tz_s.at[k], tz_r.at[k], res=zpeer(k) * NY + y)

    for k in range(1, NZ):
        tz(k).start()

    s = s1[z]
    for k in range(1, NZ):
        bz(k).wait_recv()
        s = s + b_rx[k]
    c_rx[y] = s

    def cy(k):
        return rc(c_rx.at[y], c_rx.at[y], cy_s.at[k], cy_r.at[k], res=z * NY + ypeer(k))

    for k in range(1, NY):
        cy(k).start()

    s = sm[z]
    for k in range(1, NZ):
        tz(k).wait_recv()
        s = s + t_rx[k]
    e_rx[dp] = s

    def ud(k):
        return rc(e_rx.at[dp], e_rx.at[dp], ud_s.at[k], ud_r.at[k], dp=dpeer(k))

    for k in range(1, NDP):
        ud(k).start()

    for k in range(1, NY):
        cy(k).wait_recv()
    s4[z] = ((c_rx[0] + c_rx[1] + c_rx[2] + c_rx[3]) * (1.0 / N)).astype(BF16)

    def dz(k):
        return rc(s4.at[z], s4.at[z], dz_s.at[k], dz_r.at[k], res=zpeer(k) * NY + y)

    for k in range(1, NZ):
        dz(k).start()

    for k in range(1, NDP):
        ud(k).wait_recv()
    s = e_rx[0]
    for k in range(1, NDP):
        s = s + e_rx[k]
    f_rx[y] = s

    def uy(k):
        return rc(f_rx.at[y], f_rx.at[y], uy_s.at[k], uy_r.at[k], res=z * NY + ypeer(k))

    for k in range(1, NY):
        uy(k).start()

    for k in range(1, NZ):
        dz(k).wait_recv()
    d_rx[dp] = s4[...].reshape(128, C_Z)

    def ed(k):
        return rc(d_rx.at[dp], d_rx.at[dp], ed_s.at[k], ed_r.at[k], dp=dpeer(k))

    for k in range(1, NDP):
        ed(k).start()

    for k in range(1, NY):
        uy(k).wait_recv()
    sm_out[z] = (f_rx[0] + f_rx[1] + f_rx[2] + f_rx[3]) * (1.0 / N)

    def uz(k):
        return rc(sm_out.at[z], sm_out.at[z], uz_s.at[k], uz_r.at[k], res=zpeer(k) * NY + y)

    for k in range(1, NZ):
        uz(k).start()

    for b in range(PAIRED // 16):
        src = jnp.concatenate([ract[r * SLOTS + b * 16:r * SLOTS + b * 16 + 16, :] for r in range(ROWS)], axis=0)
        agrad_ref[b * 128:(b + 1) * 128, :] = dot(perm0, src, TN).astype(BF16)
    src = jnp.concatenate([ract[r * SLOTS + PAIRED:(r + 1) * SLOTS, :] for r in range(ROWS)], axis=0)
    agrad_ref[PAIRED * ROWS:, :] = dot(pick, src, TN).astype(BF16)

    for k in range(1, NZ):
        uz(k).wait_recv()
    small_ref[...] = sm_out[...]
    for k in range(1, NDP):
        ed(k).wait_recv()
    for d in range(NDP):
        for a in range(4):
            dw_ref[:, d * 4 + a, :] = d_rx[d, a * 32:(a + 1) * 32, :].astype(F32)

    for k in range(1, NZ):
        for c in (agz, rsz, bz, tz, dz, uz):
            c(k).wait_send()
    for k in range(1, NDP):
        for c in (pdp, ud, ed):
            c(k).wait_send()
    for k in range(1, NY):
        cy(k).wait_send()
        uy(k).wait_send()
        for kz in range(NZ):
            agy(k, kz).wait_send()
            rsy(k, kz).wait_send()


def body(
    alignment, chain_ids, row_counts, norm_gain, norm_shift, left_weight, left_bias,
    right_weight, right_bias, out_weight, out_bias, pair_cotangent,
):
    wt = jnp.concatenate([left_weight, right_weight], axis=1).T
    bias = jnp.concatenate([left_bias, right_bias])
    vm = pl.BlockSpec(memory_space=pltpu.VMEM)
    sm = pl.BlockSpec(memory_space=pltpu.SMEM)
    sems = lambda *shape: pltpu.SemaphoreType.DMA(shape)
    vmem = pltpu.VMEM
    scratch = [
        vmem((ENT, C_M), F32), vmem((ENT, C_M), BF16), vmem((ENT, 1), F32),
        vmem((ENT, C_H), BF16), vmem((C_H, ENT), BF16), vmem((256, 128), BF16),
        vmem((2048, 1024), BF16), vmem((512, 1024), BF16), vmem((N, 1024), BF16), vmem((N, 1024), BF16),
        vmem((NRES, 16, 1280), BF16), vmem((NRES, 16, 1280), BF16), vmem((N, 2048), BF16), vmem((N, 512), BF16),
        vmem((NY, NZ, 16, 1280), BF16), vmem((NZ, 16, 1280), BF16), vmem((NZ, 16, 1280), BF16),
        vmem((ENT, 4096), BF16),
        vmem((NDP, 128, C_Z), F32), vmem((NDP, 128, C_Z), BF16), vmem((NDP, 128, C_Z), BF16),
        vmem((NZ, 16, C_Z), F32), vmem((NZ, 16, C_Z), F32), vmem((NY, 16, C_Z), F32), vmem((16, C_Z), BF16),
        vmem((NZ, 16, C_Z), BF16), vmem((NDP, 128, C_Z), BF16),
        vmem((NZ, 24, C_Z), F32), vmem((NZ, 24, C_Z), F32), vmem((24, C_Z), F32), vmem((NDP, 24, C_Z), F32),
        vmem((24, C_Z), F32), vmem((NY, 24, C_Z), F32), vmem((24, C_Z), F32), vmem((NZ, 24, C_Z), F32),
        vmem((ENT, C_M), BF16),
        sems(NZ), sems(NZ), sems(NY, NZ), sems(NY, NZ), sems(NY, NZ), sems(NY, NZ), sems(NZ), sems(NZ),
        sems(NDP), sems(NDP), sems(NZ), sems(NZ), sems(NY), sems(NY), sems(NZ), sems(NZ), sems(NDP), sems(NDP),
        sems(NZ), sems(NZ), sems(NDP), sems(NDP), sems(NY), sems(NY), sems(NZ), sems(NZ),
    ]
    upd, agrad, dw, small = pl.pallas_call(
        kernel,
        out_shape=(
            jax.ShapeDtypeStruct((ROWS, N, C_Z), BF16),
            jax.ShapeDtypeStruct((128 * ROWS, C_M), BF16),
            jax.ShapeDtypeStruct((C_H, C_H, C_Z), F32),
            jax.ShapeDtypeStruct((NZ, 24, C_Z), F32),
        ),
        in_specs=[sm, sm] + [vm] * 10,
        out_specs=(vm,) * 4,
        scratch_shapes=scratch,
        compiler_params=pltpu.CompilerParams(
            collective_id=0, has_side_effects=True, vmem_limit_bytes=50 * 1024 * 1024
        ),
    )(
        chain_ids, row_counts, chain_ids, alignment.reshape(128 * ROWS, C_M),
        norm_gain.reshape(1, C_M), norm_shift.reshape(1, C_M), wt,
        bias.reshape(2, C_H), bias.reshape(2 * C_H, 1),
        out_weight.reshape(C_H, C_H * C_Z), out_bias.reshape(1, C_Z), pair_cotangent[0],
    )
    flat = small.reshape(192, C_Z)
    gw = jnp.concatenate([flat[0:64], flat[64:128]], axis=1).T
    return (
        upd[None],
        agrad.reshape(1, 128, ROWS, C_M),
        gw[:, 0:C_H],
        flat[133, 0:C_H],
        gw[:, C_H:],
        flat[133, C_H:2 * C_H],
        dw.reshape(C_H * C_H, C_Z),
        flat[132],
        flat[128:130].reshape(C_M),
        flat[130:132].reshape(C_M),
    )


def solution(mesh):
    return jax.shard_map(
        body,
        mesh=mesh,
        in_specs=(
            P("dp", None, "res", None), P("dp", None), P("dp", None), P(), P(), P(), P(), P(), P(), P(), P(),
            P("dp", "res", None, None),
        ),
        out_specs=(
            P("dp", "res", None, None), P("dp", None, "res", None), P(), P(), P(), P(), P(), P(), P(), P(),
        ),
        check_vma=False,
    )
```

time: 953 us -> 80.6 us (0.08)
  waiting for transfers between devices: 788 us -> 0 us
  Pallas kernels: 0 us -> 71 us
  local copies, waits for them, and re-layouts: 79.1 us -> 8.38 us
  other arithmetic: 37.6 us -> 0.16 us
  matrix products: 31.1 us -> 0 us
  between operations: 14.2 us -> 0.74 us
    psum x2 -> x0, waiting for transfers between devices: 497 us -> none  [body(): lax.psum((left_weight_grad, left_bias_grad, right_weight_grad, right_bias...]
    reduce_scatter x1 -> x0, waiting for transfers between devices: 213 us -> none  [body(): lax.psum_scatter(column_terms.reshape(residues, kept, C_H).astype(jnp.bfl...]
    all_gather x1 -> x0, waiting for transfers between devices: 76.9 us -> none  [body(): right_all = lax.all_gather(right_rows, 'res', axis=1, tiled=True)]
    pallas_call x0 -> x1, Pallas kernels: none -> 71 us  [body(): pl.pallas_call(kernel, out_shape=(jax.ShapeDtypeStruct((ROWS, N, C_Z), BF...]
    add x6 -> x0, local copies, waits for them, and re-layouts: 33.1 us -> none  [the longest x4 32.7 us: column_step(): products = paired_prod + unpaired_prod * factor_block[:, :, None, None]]
    dot_general x24 -> x0, matrix products: 31.1 us -> none  [the longest x4 6.76 us: outer_block(): lax.dot_general(left_part.reshape(count, rows_i * C_H), right_part.reshap...]
    convert_element_type x6 -> x0, other arithmetic: 22.5 us -> none  [the longest x2 19.4 us: column_step(): (products / norm_block).astype(jnp.bfloat16)]
    convert_element_type x4 -> x0, local copies, waits for them, and re-layouts: 14.3 us -> none  [the longest x2 13.9 us: column_step(): (products / norm_block).astype(jnp.bfloat16)]
  transfers between devices with their start and end apart: 4 -> 0, of which waited for: 4 -> 0; matrix products, arithmetic and copies ran while one was open for 1% -> 0% of each run, Pallas kernels for 0% -> 0%
where the time goes in v1:
time: 80.6 us; the launch traced here: 80.3 us
  Pallas kernels  71 us (88%)
  local copies, waits for them, and re-layouts  8.38 us (10%)
    pallas_call x1, Pallas kernels, body(): pl.pallas_call(kernel, out_shape=(jax.ShapeDtypeStruct((ROWS, N, C_Z), BF...  71 us
    unnamed x25, local copies, waits for them, and re-layouts  4.78 us

profile of v1, /device:TPU:1, one launch (start us, length us, event | category | flops | bytes accessed | tf_op | source)
XLA Modules:
  0.0 80.3 jit_solution(13195461931342223402)
XLA Ops:
  0.6 0.0 copy-start.10
  0.7 0.0 copy-start.9
  0.7 0.0 copy-start
  0.7 1.1 %reshape.61.w2_ref = bf16[32,4096]{1,0:T(8,128)(2,1)S(1)} reshape(bf16[1024,128]{1,0:T(8,128)(2,1)} %param.21) | data formatting | bytes 524288 | tf_op jit(solution)/shard_map/reshape | solution.py:501
  1.8 0.0 copy-done.10
  1.8 0.0 copy-done.9
  1.8 0.1 fusion.2
  1.9 0.0 copy-start.7
  1.9 0.0 copy-start.8
  1.9 0.1 copy.22.biascol_ref
  2.0 0.6 copy-done.7
  2.6 0.0 copy-done.8
  2.6 0.1 pad_maximum_fusion
  2.7 0.1 reshape.59.bias_ref
  2.8 0.0 copy-start.3
  2.8 0.0 copy-start.4
  2.8 0.0 copy-start.5
  2.8 0.0 copy-done
  2.8 0.7 copy-done.3
  3.5 0.0 copy-done.4
  3.5 0.0 copy-done.6
  3.5 0.0 copy-done.2
  3.5 0.0 copy-done.5
  3.5 1.0 %copy-done.1 = bf16[1,8,256,128]{3,2,1,0:T(8,128)(2,1)S(1)} copy-done((bf16[1,8,256,128]{3,2,1,0:T(8,128)(2,1)S(1)}, bf16[1,8,256,128]{3,2,1,0:T(8,128)(2,1)}, u32[]{:S(2)}) %copy-start.1) | copy-done | bytes 524312
  4.6 71.0 %shard_map.195 = (bf16[8,256,128]{2,1,0:T(8,128)(2,1)S(1)}, bf16[1024,256]{1,0:T(8,128)(2,1)S(1)}, f32[32,32,128]{2,1,0:T(8,128)S(1)}, f32[8,24,128]{2,1,0:T(8,128)S(1)}) custom-call(s32[1,256]{1,0:T(1,128)S(1)} %copy-done.2, s32[1,12]{1,0:T(1,128)S(1)} %copy-done.5, s32[1,256]{1,0:T(1,128)S(1)} %copy-done.2, bf16[1024,256]{1,0:T(8,128)(2,1)S(1)} %bitcast.25, ...), custom_call_target="tpu_custom_call" | custom-call | tf_op jit(solution)/shard_map/pallas_call | solution.py:483
  75.6 0.6 fusion.1
  76.3 0.6 slice_bitcast_fusion
  76.8 0.6 slice_bitcast_fusion.3
  77.4 0.5 slice_bitcast_fusion.2
  77.9 0.8 copy.26
  78.7 0.8 copy.27
  79.5 0.8 copy.28
  (6 shorter events, 0.0 us)
Async XLA Ops:
  0.6 1.2 %copy-start.10 = (f32[32]{0:T(128)S(1)}, f32[32]{0:T(128)}, u32[]{:S(2)}) copy-start(f32[32]{0:T(128)} %param.18) | copy-start | bytes 388
  0.7 1.2 %copy-start.9 = (f32[32]{0:T(128)S(1)}, f32[32]{0:T(128)}, u32[]{:S(2)}) copy-start(f32[32]{0:T(128)} %param.20) | copy-start | bytes 388
  0.7 2.2 %copy-start = (bf16[1,128,8,256]{3,2,1,0:T(8,128)(2,1)S(1)}, bf16[1,128,8,256]{3,2,1,0:T(8,128)(2,1)}, u32[]{:S(2)}) copy-start(bf16[1,128,8,256]{3,2,1,0:T(8,128)(2,1)} %param.12) | copy-start | bytes 1572868
  1.9 0.7 copy-start.7
  1.9 0.7 copy-start.8
  2.8 0.7 copy-start.3
  2.8 0.7 copy-start.4
  2.8 0.7 copy-start.6
  2.8 0.7 copy-start.2
  2.8 0.7 copy-start.5
  3.5 1.0 %copy-start.1 = (bf16[1,8,256,128]{3,2,1,0:T(8,128)(2,1)S(1)}, bf16[1,8,256,128]{3,2,1,0:T(8,128)(2,1)}, u32[]{:S(2)}) copy-start(bf16[1,8,256,128]{3,2,1,0:T(8,128)(2,1)} %param.23) | copy-start | bytes 1572868

commit v2 on v1

--- a/solution.py
+++ b/solution.py
@@ -23,6 +23,7 @@
 NRES = NY * NZ
 N = ROWS * NRES
 ENT = ROWS * SLOTS
+HALF = 640
 F32, BF16 = jnp.float32, jnp.bfloat16
 MESH = pl.DeviceIdType.MESH
 
@@ -44,15 +45,15 @@
 
 
 def kernel(
-    chain_s, counts_s, chain_v, x_ref, gain_ref, shift_ref, wt_ref, bias_ref, biascol_ref,
-    w2_ref, obias_ref, cot_ref,
-    upd_ref, agrad_ref, dw_ref, small_ref,
-    xc, normed, inv_ref, lrow, lt, q_ref, tp, tu, g_ref, gm_ref, v_ref, rx, rp, ru,
-    ry, vsum, rz, ucat, dwf, dws, a_rx, s1, b_rx, c_rx, s3, s4, d_rx,
-    sm, t_rx, sm1, e_rx, sm2, f_rx, sm3, sm_out, ract,
-    agz_s, agz_r, agy_s, agy_r, rsy_s, rsy_r, rsz_s, rsz_r,
+    chain_s, counts_s, chain_v, x_hbm, gain_ref, shift_ref, wt_ref, bias_ref, biascol_ref,
+    w2_ref, obias_ref, cot_hbm,
+    upd_ref, agrad_ref, dw_ref, lw_ref, rw_ref, tail_ref,
+    x_ref, cot_ref, xc, normed, inv_ref, lrow, lt, q_ref, tp, tu, g_ref, gm_ref, v_ref, rx, rp, ru,
+    ry1, ry2, vsum, rz, ucat, dwf, dws, a_rx, s1, b_rx, c_rx, s4, d_rx,
+    sm, t_rx, e_rx, so, ract,
+    in_s, agz_s, agz_r, agy_s, agy_r, agf_s, agf_r, rs1_s, rs1_r, rs2_s, rs2_r, rsz_s, rsz_r,
     p_s, p_r, bz_s, bz_r, cy_s, cy_r, dz_s, dz_r, ed_s, ed_r,
-    tz_s, tz_r, ud_s, ud_r, uy_s, uy_r, uz_s, uz_r,
+    td_s, td_r, ur_s, ur_r, wd_s, wd_r,
 ):
     me = lax.axis_index("res")
     dp = lax.axis_index("dp")
@@ -73,11 +74,17 @@
             device_id=where, device_id_type=MESH,
         )
 
+    x_in = pltpu.make_async_copy(x_hbm, x_ref, in_s.at[0])
+    x_in.start()
+    cot_in = pltpu.make_async_copy(cot_hbm, cot_ref, in_s.at[1])
+    cot_in.start()
+
     barrier = pltpu.get_barrier_semaphore()
-    for k in range(1, NZ):
-        pl.semaphore_signal(barrier, inc=1, device_id={"res": zpeer(k) * NY + y}, device_id_type=MESH)
-    for k in range(1, NY):
-        pl.semaphore_signal(barrier, inc=1, device_id={"res": z * NY + ypeer(k)}, device_id_type=MESH)
+
+    @pl.loop(1, NRES)
+    def _(k):
+        pl.semaphore_signal(barrier, inc=1, device_id={"res": (me + k) % NRES}, device_id_type=MESH)
+
     for k in range(1, NDP):
         pl.semaphore_signal(barrier, inc=1, device_id={"dp": dpeer(k)}, device_id_type=MESH)
 
@@ -101,6 +108,7 @@
         live = (row >= start[r]) & (row < start[r] + count[r])
         return jnp.where((s < PAIRED) | live, 1.0, 0.0)
 
+    x_in.wait()
     ro, co = iota((128, 128), 0), iota((128, 128), 1)
     perm0 = onehot(co == (ro % 16) * ROWS + ro // 16)
     for b in range(PAIRED // 16):
@@ -142,18 +150,40 @@
             [mixed[(8 * q + a) * 16:(8 * q + a + 1) * 16, PAIRED:SLOTS] for a in range(8)], axis=1
         ).astype(BF16)
 
-    pl.semaphore_wait(barrier, NZ + NY + NDP - 3)
+    pl.semaphore_wait(barrier, NRES + NDP - 2)
 
     def agz(k):
         return rc(rx.at[me], rx.at[me], agz_s.at[k], agz_r.at[k], res=zpeer(k) * NY + y)
 
+    def agy(d, kz):
+        slot = ((z - kz + NZ) % NZ) * NY + y
+        return rc(rx.at[slot], rx.at[slot], agy_s.at[d, kz], agy_r.at[d, kz], res=z * NY + ypeer(1 + 2 * d))
+
+    def agf(d, kz):
+        slot = ((z - kz + NZ) % NZ) * NY + ypeer(3 - 2 * d)
+        part = rx.at[slot, :, d * HALF:(d + 1) * HALF]
+        return rc(part, part, agf_s.at[d, kz], agf_r.at[d, kz], res=z * NY + ypeer(1 + 2 * d))
+
+    def spread(*turns):
+        for kz in turns:
+            if kz:
+                agz(kz).wait_recv()
+            for d in range(2):
+                agy(d, kz).start()
+
+    def forward(*turns):
+        for kz in turns:
+            for d in range(2):
+                agy(d, kz).wait_recv()
+                agf(d, kz).start()
+
+    spread(0)
     for k in (1, 7, 2, 6, 3, 5, 4):
         agz(k).start()
 
     lt[...] = jnp.transpose(lrow[...].astype(F32)).astype(BF16)
 
-    @pl.loop(0, 16)
-    def _(g):
+    def t_step(g):
         h, p = g // 8, g % 8
         t = dot(lrow[...], w2_ref[:, pl.ds(pl.multiple_of(g * 256, 256), 256)]).astype(BF16)
         rowp = pl.multiple_of((p * 2 + h) * 128, 128)
@@ -163,16 +193,13 @@
                 tp[pl.ds(rowp + a * 64, 64), i * 128:(i + 1) * 128] = t[i * SLOTS:i * SLOTS + PAIRED, a * 128:(a + 1) * 128]
                 tu[pl.ds(rowu + a * 16, 16), i * 128:(i + 1) * 128] = t[i * SLOTS + PAIRED:(i + 1) * SLOTS, a * 128:(a + 1) * 128]
 
-    def agy(k, kz):
-        slot = ((z - kz + NZ) % NZ) * NY + y
-        return rc(rx.at[slot], rx.at[slot], agy_s.at[k, kz], agy_r.at[k, kz], res=z * NY + ypeer(k))
-
-    for kz in (0, 1, 7, 2, 6, 3, 5, 4):
-        if kz:
-            agz(kz).wait_recv()
-        for k in (1, 3, 2):
-            agy(k, kz).start()
-
+    pl.loop(0, 12)(t_step)
+    spread(1, 7)
+    pl.loop(12, 16)(t_step)
+    spread(2, 6)
+    forward(0)
+
+    cot_in.wait()
     chain_col = jnp.transpose(jnp.broadcast_to(chain_v[...].astype(F32), (128, N)))
     obg = jnp.zeros((8, C_Z), F32)
     inv_own = []
@@ -186,30 +213,70 @@
         g_ref[:, i * 128:(i + 1) * 128] = g
         gm_ref[:, i * 128:(i + 1) * 128] = jnp.where(same, g.astype(F32), 0.0).astype(BF16)
 
+    spread(3, 5)
+    forward(1, 7)
+
     def put_v(v, lane):
         both = jnp.concatenate(
             [v[:, 0:128].reshape(NRES, ROWS, 128), v[:, 128:256].reshape(NRES, ROWS, 128)], axis=1
         )
         v_ref[:, :, pl.ds(lane, 128)] = both.astype(BF16)
 
-    @pl.loop(0, 8)
-    def _(p):
+    def v_step(p):
         put_v(dot(g_ref[...], tp[pl.ds(pl.multiple_of(p * 256, 256), 256), :], NT), pl.multiple_of(p * 128, 128))
 
+    def rs1(d, kz):
+        dst = zpeer(kz) * NY + ypeer(2)
+        src = v_ref.at[dst, :, d * HALF:(d + 1) * HALF]
+        return rc(src, ry1.at[d, kz], rs1_s.at[d, kz], rs1_r.at[d, kz], res=z * NY + ypeer(3 - 2 * d))
+
+    def rs2(d, kz):
+        dst = zpeer(kz) * NY + ypeer(3 - 2 * d)
+        return rc(v_ref.at[dst], ry2.at[d, kz], rs2_s.at[d, kz], rs2_r.at[d, kz], res=z * NY + ypeer(3 - 2 * d))
+
+    def rsz(k):
+        return rc(vsum.at[k], rz.at[k], rsz_s.at[k], rsz_r.at[k], res=zpeer(k) * NY + y)
+
+    def second(*turns):
+        for kz in turns:
+            for d in range(2):
+                slab = zpeer(kz) * NY + ypeer(3 - 2 * d)
+                lanes = slice(d * HALF, (d + 1) * HALF)
+                rs1(d, kz).wait_recv()
+                v_ref[slab, :, lanes] = (v_ref[slab, :, lanes].astype(F32) + ry1[d, kz].astype(F32)).astype(BF16)
+                rs2(d, kz).start()
+
+    def third(*turns):
+        for kz in turns:
+            total = v_ref[zpeer(kz) * NY + y].astype(F32)
+            for d in range(2):
+                rs2(d, kz).wait_recv()
+                total = total + ry2[d, kz].astype(F32)
+            if kz:
+                vsum[kz] = total.astype(BF16)
+                rsz(kz).start()
+        return total
+
+    pl.loop(0, 4)(v_step)
+    spread(4)
+    forward(2, 6)
+    pl.loop(4, 8)(v_step)
+    forward(3)
     for q in range(2):
         put_v(dot(gm_ref[...], tu[q * 256:(q + 1) * 256, :], NT), 1024 + q * 128)
-
-    def rsy(k, kz):
-        dst = zpeer(kz) * NY + ypeer(k)
-        return rc(v_ref.at[dst], ry.at[k, kz], rsy_s.at[k, kz], rsy_r.at[k, kz], res=z * NY + ypeer(k))
-
-    for kz in (1, 7, 2, 6, 3, 5, 4, 0):
-        for k in (1, 3, 2):
-            rsy(k, kz).start()
-
+    forward(5)
+    for kz in (4, 3, 5, 2, 6):
+        for d in range(2):
+            rs1(d, kz).start()
+    forward(4)
+    for kz in (1, 7, 0):
+        for d in range(2):
+            rs1(d, kz).start()
+
+    second(4, 3, 5)
     for kz in range(NZ):
-        for k in range(1, NY):
-            agy(k, kz).wait_recv()
+        for d in range(2):
+            agf(d, kz).wait_recv()
 
     @pl.loop(0, NRES // 2)
     def _(d):
@@ -222,8 +289,9 @@
             for q in range(2):
                 ru[rows, q * 256 + h * 128:q * 256 + (h + 1) * 128] = both[:, 1024 + q * 128:1024 + (q + 1) * 128]
 
-    @pl.loop(0, 8)
-    def _(p):
+    second(2, 6)
+
+    def u_step(p):
         u = dot(rp[:, pl.ds(pl.multiple_of(p * 256, 256), 256)], g_ref[...], TN).astype(BF16)
         for h in range(2):
             for a in range(2):
@@ -231,6 +299,11 @@
                 for i in range(ROWS):
                     ucat[i * SLOTS:i * SLOTS + PAIRED, pl.ds(lane, 128)] = u[(h * 2 + a) * 64:(h * 2 + a + 1) * 64, i * 128:(i + 1) * 128]
 
+    pl.loop(0, 3)(u_step)
+    second(1, 7, 0)
+    pl.loop(3, 6)(u_step)
+    third(4, 3, 5)
+    pl.loop(6, 8)(u_step)
     for q in range(2):
         u = dot(ru[:, q * 256:(q + 1) * 256], gm_ref[...], TN).astype(BF16)
         for h in range(2):
@@ -254,26 +327,81 @@
     for k in range(1, NDP):
         pdp(k).start()
 
-    def rsz(k):
-        return rc(vsum.at[k], rz.at[k], rsz_s.at[k], rsz_r.at[k], res=zpeer(k) * NY + y)
-
-    own = None
-    for kz in (1, 7, 2, 6, 3, 5, 4, 0):
-        total = v_ref[zpeer(kz) * NY + y].astype(F32)
-        for k in range(1, NY):
-            rsy(k, kz).wait_recv()
-            total = total + ry[k, kz].astype(F32)
-        if kz:
-            vsum[kz] = total.astype(BF16)
-            rsz(kz).start()
-        else:
-            own = total
+    third(2, 6)
 
     def left_step(k, acc):
         cols = pl.ds(pl.multiple_of(k * 512, 512), 512)
         return acc + dot(ucat[:, cols], w2_ref[:, cols], NT)
 
     lgrad = lax.fori_loop(0, 8, left_step, jnp.zeros((ENT, C_H), F32))
+    own = third(1, 7, 0)
+
+    def td(c, k):
+        return rc(sm.at[c, dpeer(k)], t_rx.at[c, k], td_s.at[c, k], td_r.at[c, k], dp=dpeer(k))
+
+    def ur(c, k):
+        return rc(e_rx.at[c, me], e_rx.at[c, me], ur_s.at[c, k], ur_r.at[c, k], res=(me + k) % NRES)
+
+    def wd(c, k):
+        return rc(so.at[c, dp], so.at[c, dp], wd_s.at[c, k], wd_r.at[c, k], dp=dpeer(k))
+
+    rows8 = iota((8, C_Z), 0)
+
+    def small_first(c, gw, tail_rows):
+        tail = jnp.zeros((8, C_Z), F32)
+        for k, row in enumerate(tail_rows):
+            tail = jnp.where(rows8 == k, row, tail)
+        main = jnp.concatenate([gw[:, 0:128], gw[:, 128:256]], axis=0).reshape(8, 8, C_Z)
+        tails = jnp.broadcast_to(tail.reshape(8, 1, C_Z), (8, 8, C_Z))
+        sm[c] = jnp.concatenate([main, tails], axis=1).astype(BF16)
+        for k in range(1, NDP):
+            td(c, k).start()
+
+    def small_second(c):
+        s = sm[c, dp].astype(F32)
+        for k in range(1, NDP):
+            td(c, k).wait_recv()
+            s = s + t_rx[c, k].astype(F32)
+        e_rx[c, me] = s.astype(BF16)
+
+        @pl.loop(1, NRES)
+        def _(k):
+            ur(c, k).start()
+
+    def small_third(c):
+        @pl.loop(1, NRES)
+        def _(k):
+            ur(c, k).wait_recv()
+
+        so[c, dp] = (jnp.sum(e_rx[c].astype(F32), axis=0) * (1.0 / N)).astype(BF16)
+        for k in range(1, NDP):
+            wd(c, k).start()
+
+    def small_last(c, gw_ref):
+        for k in range(1, NDP):
+            wd(c, k).wait_recv()
+        for d in range(NDP):
+            part = so[c, d].astype(F32)
+            sm_f = part[0:8]
+            tail_ref[c * 8 + d:c * 8 + d + 1, :] = part[8:9]
+            if d == 0:
+                blocks = []
+            blocks.append(sm_f)
+        gw_ref[0:128, :] = jnp.transpose(jnp.concatenate(blocks[0:4], axis=0))
+        gw_ref[128:256, :] = jnp.transpose(jnp.concatenate(blocks[4:8], axis=0))
+
+    gw_l = jnp.zeros((C_H, C_M), F32)
+    gb_l = jnp.zeros((1, C_H), F32)
+    for r in range(ROWS):
+        rows = slice(r * SLOTS, (r + 1) * SLOTS)
+        lact = (lgrad[rows] * slot_mask(r, (SLOTS, C_H), 0)).astype(BF16)
+        gw_l = gw_l + dot(lact, normed[rows, :], TN)
+        gb_l = gb_l + jnp.sum(lact.astype(F32), axis=0, keepdims=True)
+        lrow[rows, :] = lact
+    small_first(0, gw_l, (
+        jnp.sum(obg, axis=0, keepdims=True),
+        jnp.concatenate([gb_l, jnp.zeros((1, 96), F32)], axis=1),
+    ))
 
     @pl.loop(0, 4)
     def _(g):
@@ -304,7 +432,9 @@
     for k in range(1, NZ):
         bz(k).start()
 
-    for kz in range(1, NZ):
+    small_second(0)
+
+    for kz in (4, 3, 5, 2, 6, 1, 7):
         rsz(kz).wait_recv()
         own = own + rz[kz].astype(F32)
     tiles = []
@@ -312,50 +442,28 @@
         tiles.append(jnp.concatenate([own[:, e * 64:(e + 1) * 64], own[:, 1024 + e * 16:1024 + (e + 1) * 16]], axis=1))
     back = dot(permq, jnp.concatenate(tiles, axis=0).astype(BF16), TN)
 
-    gw_l = jnp.zeros((C_H, C_M), F32)
     gw_r = jnp.zeros((C_H, C_M), F32)
-    gb_l = jnp.zeros((1, C_H), F32)
     gb_r = jnp.zeros((C_H, 1), F32)
     gain_g = jnp.zeros((1, C_M), F32)
     shift_g = jnp.zeros((1, C_M), F32)
     for r in range(ROWS):
         rows = slice(r * SLOTS, (r + 1) * SLOTS)
-        nrm = normed[rows, :]
-        lact = (lgrad[rows] * slot_mask(r, (SLOTS, C_H), 0)).astype(BF16)
         ract_t = (back[r * C_H:(r + 1) * C_H, :] * slot_mask(r, (C_H, SLOTS), 1)).astype(BF16)
-        gw_l = gw_l + dot(lact, nrm, TN)
-        gw_r = gw_r + dot(ract_t, nrm)
-        gb_l = gb_l + jnp.sum(lact.astype(F32), axis=0, keepdims=True)
+        gw_r = gw_r + dot(ract_t, normed[rows, :])
         gb_r = gb_r + jnp.sum(ract_t.astype(F32), axis=1, keepdims=True)
-        gn = dot(lact, wt_ref[0:C_H, :]) + dot(ract_t, wt_ref[C_H:, :], TN)
+        gn = dot(lrow[rows, :], wt_ref[0:C_H, :]) + dot(ract_t, wt_ref[C_H:, :], TN)
         scaled = xc[rows, :]
-        gs = gn * scaled
-        gain_g = gain_g + jnp.sum(gs, axis=0, keepdims=True)
+        gain_g = gain_g + jnp.sum(gn * scaled, axis=0, keepdims=True)
         shift_g = shift_g + jnp.sum(gn, axis=0, keepdims=True)
         gg = gn * gain_ref[...]
         mean_g = jnp.mean(gg, axis=-1, keepdims=True)
         mean_p = jnp.mean(gg * scaled, axis=-1, keepdims=True)
         ract[rows, :] = (inv_ref[rows, :] * (gg - mean_g - scaled * mean_p)).astype(BF16)
-
-    smf = jnp.concatenate([gw_l, gw_r], axis=0)
     gbr_row = jnp.transpose(jnp.broadcast_to(gb_r, (C_H, 128)))[0:1, :]
-    rows8 = iota((8, C_Z), 0)
-    tail = jnp.zeros((8, C_Z), F32)
-    tail_rows = (
+    small_first(1, gw_r, (
         gain_g[:, 0:128], gain_g[:, 128:256], shift_g[:, 0:128], shift_g[:, 128:256],
-        jnp.sum(obg, axis=0, keepdims=True),
-        jnp.concatenate([gb_l, gbr_row, jnp.zeros((1, 64), F32)], axis=1),
-    )
-    for k, row in enumerate(tail_rows):
-        tail = jnp.where(rows8 == k, row, tail)
-    flat = jnp.concatenate([smf[:, 0:128], smf[:, 128:256], tail, jnp.zeros((56, C_Z), F32)], axis=0)
-    sm[...] = flat.reshape(NZ, 24, C_Z)
-
-    def tz(k):
-        return rc(sm.at[zpeer(k)], t_rx.at[k], tz_s.at[k], tz_r.at[k], res=zpeer(k) * NY + y)
-
-    for k in range(1, NZ):
-        tz(k).start()
+        jnp.concatenate([gbr_row, jnp.zeros((1, 96), F32)], axis=1),
+    ))
 
     s = s1[z]
     for k in range(1, NZ):
@@ -369,17 +477,7 @@
     for k in range(1, NY):
         cy(k).start()
 
-    s = sm[z]
-    for k in range(1, NZ):
-        tz(k).wait_recv()
-        s = s + t_rx[k]
-    e_rx[dp] = s
-
-    def ud(k):
-        return rc(e_rx.at[dp], e_rx.at[dp], ud_s.at[k], ud_r.at[k], dp=dpeer(k))
-
-    for k in range(1, NDP):
-        ud(k).start()
+    small_second(1)
 
     for k in range(1, NY):
         cy(k).wait_recv()
@@ -391,38 +489,7 @@
     for k in range(1, NZ):
         dz(k).start()
 
-    for k in range(1, NDP):
-        ud(k).wait_recv()
-    s = e_rx[0]
-    for k in range(1, NDP):
-        s = s + e_rx[k]
-    f_rx[y] = s
-
-    def uy(k):
-        return rc(f_rx.at[y], f_rx.at[y], uy_s.at[k], uy_r.at[k], res=z * NY + ypeer(k))
-
-    for k in range(1, NY):
-        uy(k).start()
-
-    for k in range(1, NZ):
-        dz(k).wait_recv()
-    d_rx[dp] = s4[...].reshape(128, C_Z)
-
-    def ed(k):
-        return rc(d_rx.at[dp], d_rx.at[dp], ed_s.at[k], ed_r.at[k], dp=dpeer(k))
-
-    for k in range(1, NDP):
-        ed(k).start()
-
-    for k in range(1, NY):
-        uy(k).wait_recv()
-    sm_out[z] = (f_rx[0] + f_rx[1] + f_rx[2] + f_rx[3]) * (1.0 / N)
-
-    def uz(k):
-        return rc(sm_out.at[z], sm_out.at[z], uz_s.at[k], uz_r.at[k], res=zpeer(k) * NY + y)
-
-    for k in range(1, NZ):
-        uz(k).start()
+    small_third(0)
 
     for b in range(PAIRED // 16):
         src = jnp.concatenate([ract[r * SLOTS + b * 16:r * SLOTS + b * 16 + 16, :] for r in range(ROWS)], axis=0)
@@ -431,26 +498,44 @@
     agrad_ref[PAIRED * ROWS:, :] = dot(pick, src, TN).astype(BF16)
 
     for k in range(1, NZ):
-        uz(k).wait_recv()
-    small_ref[...] = sm_out[...]
+        dz(k).wait_recv()
+    d_rx[dp] = s4[...].reshape(128, C_Z)
+
+    def ed(k):
+        return rc(d_rx.at[dp], d_rx.at[dp], ed_s.at[k], ed_r.at[k], dp=dpeer(k))
+
+    for k in range(1, NDP):
+        ed(k).start()
+
+    small_third(1)
+    small_last(0, lw_ref)
     for k in range(1, NDP):
         ed(k).wait_recv()
     for d in range(NDP):
         for a in range(4):
             dw_ref[:, d * 4 + a, :] = d_rx[d, a * 32:(a + 1) * 32, :].astype(F32)
 
+    small_last(1, rw_ref)
+
     for k in range(1, NZ):
-        for c in (agz, rsz, bz, tz, dz, uz):
+        for c in (agz, rsz, bz, dz):
             c(k).wait_send()
     for k in range(1, NDP):
-        for c in (pdp, ud, ed):
+        for c in (pdp, ed):
             c(k).wait_send()
+        for c in range(2):
+            td(c, k).wait_send()
+            wd(c, k).wait_send()
+    for c in range(2):
+        @pl.loop(1, NRES)
+        def _(k):
+            ur(c, k).wait_send()
     for k in range(1, NY):
         cy(k).wait_send()
-        uy(k).wait_send()
-        for kz in range(NZ):
-            agy(k, kz).wait_send()
-            rsy(k, kz).wait_send()
+    for kz in range(NZ):
+        for d in range(2):
+            for c in (agy, agf, rs1, rs2):
+                c(d, kz).wait_send()
 
 
 def body(
@@ -464,32 +549,36 @@
     sems = lambda *shape: pltpu.SemaphoreType.DMA(shape)
     vmem = pltpu.VMEM
     scratch = [
+        vmem((128 * ROWS, C_M), BF16), vmem((ROWS, N, C_Z), BF16),
         vmem((ENT, C_M), F32), vmem((ENT, C_M), BF16), vmem((ENT, 1), F32),
         vmem((ENT, C_H), BF16), vmem((C_H, ENT), BF16), vmem((256, 128), BF16),
         vmem((2048, 1024), BF16), vmem((512, 1024), BF16), vmem((N, 1024), BF16), vmem((N, 1024), BF16),
         vmem((NRES, 16, 1280), BF16), vmem((NRES, 16, 1280), BF16), vmem((N, 2048), BF16), vmem((N, 512), BF16),
-        vmem((NY, NZ, 16, 1280), BF16), vmem((NZ, 16, 1280), BF16), vmem((NZ, 16, 1280), BF16),
+        vmem((2, NZ, 16, HALF), BF16), vmem((2, NZ, 16, 1280), BF16), vmem((NZ, 16, 1280), BF16), vmem((NZ, 16, 1280), BF16),
         vmem((ENT, 4096), BF16),
         vmem((NDP, 128, C_Z), F32), vmem((NDP, 128, C_Z), BF16), vmem((NDP, 128, C_Z), BF16),
-        vmem((NZ, 16, C_Z), F32), vmem((NZ, 16, C_Z), F32), vmem((NY, 16, C_Z), F32), vmem((16, C_Z), BF16),
+        vmem((NZ, 16, C_Z), F32), vmem((NZ, 16, C_Z), F32), vmem((NY, 16, C_Z), F32),
         vmem((NZ, 16, C_Z), BF16), vmem((NDP, 128, C_Z), BF16),
-        vmem((NZ, 24, C_Z), F32), vmem((NZ, 24, C_Z), F32), vmem((24, C_Z), F32), vmem((NDP, 24, C_Z), F32),
-        vmem((24, C_Z), F32), vmem((NY, 24, C_Z), F32), vmem((24, C_Z), F32), vmem((NZ, 24, C_Z), F32),
+        vmem((2, NDP, 16, C_Z), BF16), vmem((2, NDP, 16, C_Z), BF16), vmem((2, NRES, 16, C_Z), BF16), vmem((2, NDP, 16, C_Z), BF16),
         vmem((ENT, C_M), BF16),
-        sems(NZ), sems(NZ), sems(NY, NZ), sems(NY, NZ), sems(NY, NZ), sems(NY, NZ), sems(NZ), sems(NZ),
+        sems(2), sems(NZ), sems(NZ), sems(2, NZ), sems(2, NZ), sems(2, NZ), sems(2, NZ),
+        sems(2, NZ), sems(2, NZ), sems(2, NZ), sems(2, NZ), sems(NZ), sems(NZ),
         sems(NDP), sems(NDP), sems(NZ), sems(NZ), sems(NY), sems(NY), sems(NZ), sems(NZ), sems(NDP), sems(NDP),
-        sems(NZ), sems(NZ), sems(NDP), sems(NDP), sems(NY), sems(NY), sems(NZ), sems(NZ),
+        sems(2, NDP), sems(2, NDP), sems(2, NRES), sems(2, NRES), sems(2, NDP), sems(2, NDP),
     ]
-    upd, agrad, dw, small = pl.pallas_call(
+    hbm = pl.BlockSpec(memory_space=pl.ANY)
+    upd, agrad, dw, lw, rw, tails = pl.pallas_call(
         kernel,
         out_shape=(
             jax.ShapeDtypeStruct((ROWS, N, C_Z), BF16),
             jax.ShapeDtypeStruct((128 * ROWS, C_M), BF16),
             jax.ShapeDtypeStruct((C_H, C_H, C_Z), F32),
-            jax.ShapeDtypeStruct((NZ, 24, C_Z), F32),
+            jax.ShapeDtypeStruct((C_M, C_H), F32),
+            jax.ShapeDtypeStruct((C_M, C_H), F32),
+            jax.ShapeDtypeStruct((16, C_Z), F32),
         ),
-        in_specs=[sm, sm] + [vm] * 10,
-        out_specs=(vm,) * 4,
+        in_specs=[sm, sm, vm, hbm] + [vm] * 7 + [hbm],
+        out_specs=(vm,) * 6,
         scratch_shapes=scratch,
         compiler_params=pltpu.CompilerParams(
             collective_id=0, has_side_effects=True, vmem_limit_bytes=50 * 1024 * 1024
@@ -500,19 +589,17 @@
         bias.reshape(2, C_H), bias.reshape(2 * C_H, 1),
         out_weight.reshape(C_H, C_H * C_Z), out_bias.reshape(1, C_Z), pair_cotangent[0],
     )
-    flat = small.reshape(192, C_Z)
-    gw = jnp.concatenate([flat[0:64], flat[64:128]], axis=1).T
     return (
         upd[None],
         agrad.reshape(1, 128, ROWS, C_M),
-        gw[:, 0:C_H],
-        flat[133, 0:C_H],
-        gw[:, C_H:],
-        flat[133, C_H:2 * C_H],
+        lw,
+        tails[1, 0:C_H],
+        rw,
+        tails[12, 0:C_H],
         dw.reshape(C_H * C_H, C_Z),
-        flat[132],
-        flat[128:130].reshape(C_M),
-        flat[130:132].reshape(C_M),
+        tails[0],
+        tails[8:10].reshape(C_M),
+        tails[10:12].reshape(C_M),
     )
 
 

time: 80.6 us -> 79 us (0.980)
  Pallas kernels: 71 us -> 68.8 us
    pallas_call x1, Pallas kernels: 71 us -> 68.8 us  [body(): pl.pallas_call(kernel, out_shape=(jax.ShapeDtypeStruct((ROWS, N, C_Z), BF...]
    unnamed x25 -> x27, local copies, waits for them, and re-layouts: 4.78 us -> 6.15 us
where the time goes in v2:
time: 79 us; the launch traced here: 78.8 us
  Pallas kernels  68.8 us (87%)
  local copies, waits for them, and re-layouts  9.06 us (11%)
    pallas_call x1, Pallas kernels, body(): pl.pallas_call(kernel, out_shape=(jax.ShapeDtypeStruct((ROWS, N, C_Z), BF...  68.8 us
    unnamed x27, local copies, waits for them, and re-layouts  6.15 us

profile of v2, /device:TPU:1, one launch (start us, length us, event | category | flops | bytes accessed | tf_op | source)
XLA Modules:
  0.0 78.8 jit_solution(2504868446583746165)
XLA Ops:
  0.6 0.0 copy-start.10
  0.7 0.0 copy-start.9
  0.7 0.0 copy-start
  0.7 1.1 %reshape.58.w2_ref = bf16[32,4096]{1,0:T(8,128)(2,1)S(1)} reshape(bf16[1024,128]{1,0:T(8,128)(2,1)} %param.21) | data formatting | bytes 524288 | tf_op jit(solution)/shard_map/reshape | solution.py:590
  1.8 0.0 copy-done.10
  1.8 0.0 copy-done.9
  1.8 0.1 fusion
  1.9 0.0 copy-start.7
  1.9 0.0 copy-start.8
  1.9 0.1 copy.22.biascol_ref
  2.0 0.6 copy-done.7
  2.6 0.0 copy-done.8
  2.6 0.1 pad_maximum_fusion
  2.7 0.1 reshape.56.bias_ref
  2.8 0.0 copy-start.3
  2.8 0.0 copy-start.5
  2.8 0.0 copy-done
  2.8 0.7 copy-done.3
  3.5 0.0 copy-done.4
  3.5 0.0 copy-done.6
  3.5 0.0 copy-done.2
  3.5 0.0 copy-done.5
  3.5 1.0 %copy-done.1 = bf16[1,8,256,128]{3,2,1,0:T(8,128)(2,1)S(1)} copy-done((bf16[1,8,256,128]{3,2,1,0:T(8,128)(2,1)S(1)}, bf16[1,8,256,128]{3,2,1,0:T(8,128)(2,1)}, u32[]{:S(2)}) %copy-start.1) | copy-done | bytes 524312
  4.6 68.8 %shard_map.195 = (bf16[8,256,128]{2,1,0:T(8,128)(2,1)S(1)}, bf16[1024,256]{1,0:T(8,128)(2,1)S(1)}, f32[32,32,128]{2,1,0:T(8,128)S(1)}, f32[256,32]{1,0:T(8,128)S...) custom-call(s32[1,256]{1,0:T(1,128)S(1)} %copy-done.2, s32[1,12]{1,0:T(1,128)S(1)} %copy-done.5, ...), custom_call_target="tpu_custom_call" | custom-call | tf_op jit(solution)/shard_map/pallas_call | solution.py:570
  73.4 0.6 slice_bitcast_fusion
  74.0 0.5 slice_bitcast_fusion.3
  74.5 0.5 slice_bitcast_fusion.2
  75.0 0.7 copy.23
  75.7 0.7 copy.24
  76.4 0.8 %copy.28 = bf16[1,8,256,128]{3,2,1,0:T(8,128)(2,1)} copy(bf16[1,8,256,128]{3,2,1,0:T(8,128)(2,1)S(1)} %bitcast.26) | data formatting | bytes 1048576
  77.2 0.8 %copy.29 = bf16[1,128,8,256]{3,2,1,0:T(8,128)(2,1)} copy(bf16[1,128,8,256]{3,2,1,0:T(8,128)(2,1)S(1)} %bitcast.25) | data formatting | bytes 1048576
  78.0 0.8 %copy.30 = f32[1024,128]{1,0:T(8,128)} copy(f32[1024,128]{1,0:T(8,128)S(1)} %bitcast.24) | data formatting | bytes 1048576
  (5 shorter events, 0.0 us)
Async XLA Ops:
  0.6 1.2 %copy-start.10 = (f32[32]{0:T(128)S(1)}, f32[32]{0:T(128)}, u32[]{:S(2)}) copy-start(f32[32]{0:T(128)} %param.18) | copy-start | bytes 388
  0.7 1.2 %copy-start.9 = (f32[32]{0:T(128)S(1)}, f32[32]{0:T(128)}, u32[]{:S(2)}) copy-start(f32[32]{0:T(128)} %param.20) | copy-start | bytes 388
  0.7 2.2 %copy-start = (bf16[1,128,8,256]{3,2,1,0:T(8,128)(2,1)S(1)}, bf16[1,128,8,256]{3,2,1,0:T(8,128)(2,1)}, u32[]{:S(2)}) copy-start(bf16[1,128,8,256]{3,2,1,0:T(8,128)(2,1)} %param.12) | copy-start | bytes 1572868
  1.9 0.7 copy-start.7
  1.9 0.7 copy-start.8
  2.8 0.7 copy-start.3
  2.8 0.7 copy-start.4
  2.8 0.7 copy-start.6
  2.8 0.7 copy-start.2
  2.8 0.7 copy-start.5
  3.5 1.0 %copy-start.1 = (bf16[1,8,256,128]{3,2,1,0:T(8,128)(2,1)S(1)}, bf16[1,8,256,128]{3,2,1,0:T(8,128)(2,1)}, u32[]{:S(2)}) copy-start(bf16[1,8,256,128]{3,2,1,0:T(8,128)(2,1)} %param.23) | copy-start | bytes 1572868

commit v3 on v2

--- a/solution.py
+++ b/solution.py
@@ -45,13 +45,14 @@
 
 
 def kernel(
-    chain_s, counts_s, chain_v, x_hbm, gain_ref, shift_ref, wt_ref, bias_ref, biascol_ref,
-    w2_ref, obias_ref, cot_hbm,
-    upd_ref, agrad_ref, dw_ref, lw_ref, rw_ref, tail_ref,
-    x_ref, cot_ref, xc, normed, inv_ref, lrow, lt, q_ref, tp, tu, g_ref, gm_ref, v_ref, rx, rp, ru,
+    chain_h, counts_h, x_h, gain_h, shift_h, lw_h, lb_h, rw_h, rb_h, w_h, ob_h, cot_h,
+    upd_h, agrad_h, dw_h, small_h,
+    upd_ref, agrad_ref, chain_s, counts_s, chain_v, x_ref, gain_ref, shift_ref, lb_ref, rb_ref, w_ref, obias_ref, cot_ref,
+    wt_ref, wf, w2_ref,
+    xc, normed, inv_ref, lrow, lt, q_ref, tp, tu, g_ref, gm_ref, v_ref, rx, rp, ru,
     ry1, ry2, vsum, rz, ucat, dwf, dws, a_rx, s1, b_rx, c_rx, s4, d_rx,
     sm, t_rx, e_rx, so, ract,
-    in_s, agz_s, agz_r, agy_s, agy_r, agf_s, agf_r, rs1_s, rs1_r, rs2_s, rs2_r, rsz_s, rsz_r,
+    in_s, out_s, agz_s, agz_r, agy_s, agy_r, agf_s, agf_r, rs1_s, rs1_r, rs2_s, rs2_r, rsz_s, rsz_r,
     p_s, p_r, bz_s, bz_r, cy_s, cy_r, dz_s, dz_r, ed_s, ed_r,
     td_s, td_r, ur_s, ur_r, wd_s, wd_r,
 ):
@@ -74,10 +75,16 @@
             device_id=where, device_id_type=MESH,
         )
 
-    x_in = pltpu.make_async_copy(x_hbm, x_ref, in_s.at[0])
-    x_in.start()
-    cot_in = pltpu.make_async_copy(cot_hbm, cot_ref, in_s.at[1])
-    cot_in.start()
+    fetches = [
+        pltpu.make_async_copy(src, dst, in_s.at[n])
+        for n, (src, dst) in enumerate((
+            (x_h, x_ref), (chain_h, chain_s), (counts_h, counts_s), (chain_h, chain_v), (gain_h, gain_ref),
+            (shift_h, shift_ref), (lw_h, wt_ref.at[0:C_H]), (lb_h, lb_ref), (rw_h, wt_ref.at[C_H:2 * C_H]), (rb_h, rb_ref),
+            (w_h, w_ref), (ob_h, obias_ref), (cot_h, cot_ref),
+        ))
+    ]
+    for f in fetches:
+        f.start()
 
     barrier = pltpu.get_barrier_semaphore()
 
@@ -87,6 +94,10 @@
 
     for k in range(1, NDP):
         pl.semaphore_signal(barrier, inc=1, device_id={"dp": dpeer(k)}, device_id_type=MESH)
+
+    for f in fetches[:10]:
+        f.wait()
+    rb_col = jnp.transpose(jnp.broadcast_to(rb_ref[...], (8, C_H)))[:, 0:1]
 
     chain, start, count, base = [], [], [], []
     for r in range(ROWS):
@@ -108,7 +119,6 @@
         live = (row >= start[r]) & (row < start[r] + count[r])
         return jnp.where((s < PAIRED) | live, 1.0, 0.0)
 
-    x_in.wait()
     ro, co = iota((128, 128), 0), iota((128, 128), 1)
     perm0 = onehot(co == (ro % 16) * ROWS + ro // 16)
     for b in range(PAIRED // 16):
@@ -134,9 +144,9 @@
         xc[rows, :] = scaled
         inv_ref[rows, :] = inverse
         normed[rows, :] = nrm
-        left = (dot(nrm, wt_ref[0:C_H, :], NT) + bias_ref[0:1, :]) * slot_mask(r, (SLOTS, C_H), 0)
+        left = (dot(nrm, wt_ref[0:C_H, :], NT) + lb_ref[...]) * slot_mask(r, (SLOTS, C_H), 0)
         lrow[rows, :] = left.astype(BF16)
-        right = (dot(wt_ref[C_H:, :], nrm, NT) + biascol_ref[C_H:, :]) * slot_mask(r, (C_H, SLOTS), 1)
+        right = (dot(wt_ref[C_H:, :], nrm, NT) + rb_col) * slot_mask(r, (C_H, SLOTS), 1)
         q_ref[r * C_H:(r + 1) * C_H, 0:SLOTS] = right.astype(BF16)
     re, ce = iota((256, 256), 0), iota((256, 256), 1)
     permq = onehot(ce == (re % 8) * 32 + ((re // 8) % 2) * 16 + re // 16)
@@ -181,6 +191,12 @@
     for k in (1, 7, 2, 6, 3, 5, 4):
         agz(k).start()
 
+    for f in fetches[10:]:
+        f.wait()
+    wf[...] = w_ref[...].astype(F32)
+    for e in range(C_H):
+        w2_ref[:, e * 128:(e + 1) * 128] = wf[pl.ds(e, C_H, stride=C_H), :].astype(BF16)
+
     lt[...] = jnp.transpose(lrow[...].astype(F32)).astype(BF16)
 
     def t_step(g):
@@ -199,7 +215,6 @@
     spread(2, 6)
     forward(0)
 
-    cot_in.wait()
     chain_col = jnp.transpose(jnp.broadcast_to(chain_v[...].astype(F32), (128, N)))
     obg = jnp.zeros((8, C_Z), F32)
     inv_own = []
@@ -273,7 +288,6 @@
         for d in range(2):
             rs1(d, kz).start()
 
-    second(4, 3, 5)
     for kz in range(NZ):
         for d in range(2):
             agf(d, kz).wait_recv()
@@ -289,8 +303,6 @@
             for q in range(2):
                 ru[rows, q * 256 + h * 128:q * 256 + (h + 1) * 128] = both[:, 1024 + q * 128:1024 + (q + 1) * 128]
 
-    second(2, 6)
-
     def u_step(p):
         u = dot(rp[:, pl.ds(pl.multiple_of(p * 256, 256), 256)], g_ref[...], TN).astype(BF16)
         for h in range(2):
@@ -300,9 +312,9 @@
                     ucat[i * SLOTS:i * SLOTS + PAIRED, pl.ds(lane, 128)] = u[(h * 2 + a) * 64:(h * 2 + a + 1) * 64, i * 128:(i + 1) * 128]
 
     pl.loop(0, 3)(u_step)
-    second(1, 7, 0)
+    second(4, 3, 5)
     pl.loop(3, 6)(u_step)
-    third(4, 3, 5)
+    second(2, 6, 1)
     pl.loop(6, 8)(u_step)
     for q in range(2):
         u = dot(ru[:, q * 256:(q + 1) * 256], gm_ref[...], TN).astype(BF16)
@@ -312,6 +324,9 @@
                 for i in range(ROWS):
                     ucat[i * SLOTS + PAIRED:(i + 1) * SLOTS, lane:lane + 128] = u[(h * 8 + a) * 16:(h * 8 + a + 1) * 16, i * 128:(i + 1) * 128]
 
+    second(7, 0)
+    third(4, 3, 5)
+
     @pl.loop(0, 16)
     def _(g):
         dw = dot(lt[...], ucat[:, pl.ds(pl.multiple_of(g * 256, 256), 256)])
@@ -327,20 +342,19 @@
     for k in range(1, NDP):
         pdp(k).start()
 
-    third(2, 6)
+    own = third(2, 6, 1, 7, 0)
 
     def left_step(k, acc):
         cols = pl.ds(pl.multiple_of(k * 512, 512), 512)
         return acc + dot(ucat[:, cols], w2_ref[:, cols], NT)
 
     lgrad = lax.fori_loop(0, 8, left_step, jnp.zeros((ENT, C_H), F32))
-    own = third(1, 7, 0)
 
     def td(c, k):
         return rc(sm.at[c, dpeer(k)], t_rx.at[c, k], td_s.at[c, k], td_r.at[c, k], dp=dpeer(k))
 
     def ur(c, k):
-        return rc(e_rx.at[c, me], e_rx.at[c, me], ur_s.at[c, k], ur_r.at[c, k], res=(me + k) % NRES)
+        return rc(e_rx.at[c, me], e_rx.at[c, me], ur_s.at[c], ur_r.at[c], res=(me + k) % NRES)
 
     def wd(c, k):
         return rc(so.at[c, dp], so.at[c, dp], wd_s.at[c, k], wd_r.at[c, k], dp=dpeer(k))
@@ -369,26 +383,12 @@
             ur(c, k).start()
 
     def small_third(c):
-        @pl.loop(1, NRES)
-        def _(k):
-            ur(c, k).wait_recv()
+        others = e_rx.at[c, 0:NRES - 1]
+        rc(others, others, ur_s.at[c], ur_r.at[c], res=(me + 1) % NRES).wait()
 
         so[c, dp] = (jnp.sum(e_rx[c].astype(F32), axis=0) * (1.0 / N)).astype(BF16)
         for k in range(1, NDP):
             wd(c, k).start()
-
-    def small_last(c, gw_ref):
-        for k in range(1, NDP):
-            wd(c, k).wait_recv()
-        for d in range(NDP):
-            part = so[c, d].astype(F32)
-            sm_f = part[0:8]
-            tail_ref[c * 8 + d:c * 8 + d + 1, :] = part[8:9]
-            if d == 0:
-                blocks = []
-            blocks.append(sm_f)
-        gw_ref[0:128, :] = jnp.transpose(jnp.concatenate(blocks[0:4], axis=0))
-        gw_ref[128:256, :] = jnp.transpose(jnp.concatenate(blocks[4:8], axis=0))
 
     gw_l = jnp.zeros((C_H, C_M), F32)
     gb_l = jnp.zeros((1, C_H), F32)
@@ -402,23 +402,6 @@
         jnp.sum(obg, axis=0, keepdims=True),
         jnp.concatenate([gb_l, jnp.zeros((1, 96), F32)], axis=1),
     ))
-
-    @pl.loop(0, 4)
-    def _(g):
-        cols = pl.ds(pl.multiple_of(g * 256, 256), 256)
-        main = dot(rp[...], tp[:, cols])
-        side = dot(ru[...], tu[:, cols])
-        for a in range(2):
-            i = 2 * g + a
-            ch = jnp.int32(0)
-            iv = jnp.zeros((1, C_Z), F32)
-            for r in range(ROWS):
-                ch = jnp.where(i == r, chain[r], ch)
-                iv = jnp.where(i == r, inv_own[r], iv)
-            same = chain_col == ch.astype(F32)
-            m, s = main[:, a * 128:(a + 1) * 128], side[:, a * 128:(a + 1) * 128]
-            out = jnp.where(same, (m + s) * iv, m * (1.0 / (PAIRED + NORM_FLOOR))) + obias_ref[...]
-            upd_ref[i] = out.astype(BF16)
 
     s = dwf[dp]
     for k in range(1, NDP):
@@ -491,12 +474,32 @@
 
     small_third(0)
 
+    @pl.loop(0, 4)
+    def _(g):
+        cols = pl.ds(pl.multiple_of(g * 256, 256), 256)
+        main = dot(rp[...], tp[:, cols])
+        side = dot(ru[...], tu[:, cols])
+        for a in range(2):
+            i = 2 * g + a
+            ch = jnp.int32(0)
+            iv = jnp.zeros((1, C_Z), F32)
+            for r in range(ROWS):
+                ch = jnp.where(i == r, chain[r], ch)
+                iv = jnp.where(i == r, inv_own[r], iv)
+            same = chain_col == ch.astype(F32)
+            m, s = main[:, a * 128:(a + 1) * 128], side[:, a * 128:(a + 1) * 128]
+            out = jnp.where(same, (m + s) * iv, m * (1.0 / (PAIRED + NORM_FLOOR))) + obias_ref[...]
+            upd_ref[i] = out.astype(BF16)
+
     for b in range(PAIRED // 16):
         src = jnp.concatenate([ract[r * SLOTS + b * 16:r * SLOTS + b * 16 + 16, :] for r in range(ROWS)], axis=0)
         agrad_ref[b * 128:(b + 1) * 128, :] = dot(perm0, src, TN).astype(BF16)
     src = jnp.concatenate([ract[r * SLOTS + PAIRED:(r + 1) * SLOTS, :] for r in range(ROWS)], axis=0)
     agrad_ref[PAIRED * ROWS:, :] = dot(pick, src, TN).astype(BF16)
 
+    upd_out = pltpu.make_async_copy(upd_ref, upd_h, out_s.at[0])
+    upd_out.start()
+
     for k in range(1, NZ):
         dz(k).wait_recv()
     d_rx[dp] = s4[...].reshape(128, C_Z)
@@ -508,48 +511,100 @@
         ed(k).start()
 
     small_third(1)
-    small_last(0, lw_ref)
-    for k in range(1, NDP):
-        ed(k).wait_recv()
-    for d in range(NDP):
-        for a in range(4):
-            dw_ref[:, d * 4 + a, :] = d_rx[d, a * 32:(a + 1) * 32, :].astype(F32)
-
-    small_last(1, rw_ref)
-
-    for k in range(1, NZ):
-        for c in (agz, rsz, bz, dz):
-            c(k).wait_send()
-    for k in range(1, NDP):
-        for c in (pdp, ed):
-            c(k).wait_send()
-        for c in range(2):
-            td(c, k).wait_send()
-            wd(c, k).wait_send()
-    for c in range(2):
-        @pl.loop(1, NRES)
-        def _(k):
-            ur(c, k).wait_send()
-    for k in range(1, NY):
-        cy(k).wait_send()
+    agrad_out = pltpu.make_async_copy(agrad_ref, agrad_h, out_s.at[1])
+    agrad_out.start()
     for kz in range(NZ):
         for d in range(2):
             for c in (agy, agf, rs1, rs2):
                 c(d, kz).wait_send()
+    for k in range(1, NZ):
+        for c in (agz, rsz, bz, dz):
+            c(k).wait_send()
+    for k in range(1, NDP):
+        pdp(k).wait_send()
+        td(0, k).wait_send()
+        td(1, k).wait_send()
+        wd(0, k).wait_send()
+    for k in range(1, NY):
+        cy(k).wait_send()
+
+    for k in range(1, NDP):
+        wd(0, k).wait_recv()
+    small0_out = pltpu.make_async_copy(so.at[0], small_h.at[0], out_s.at[2])
+    small0_out.start()
+    for k in range(1, NDP):
+        ed(k).wait_recv()
+    dw_out = pltpu.make_async_copy(d_rx, dw_h, out_s.at[3])
+    dw_out.start()
+    for k in range(1, NDP):
+        wd(1, k).wait_recv()
+    small1_out = pltpu.make_async_copy(so.at[1], small_h.at[1], out_s.at[4])
+    small1_out.start()
+    for k in range(1, NDP):
+        ed(k).wait_send()
+        wd(1, k).wait_send()
+    for c in (upd_out, agrad_out, small0_out, dw_out, small1_out):
+        c.wait()
+
+
+def finish(
+    upd_i, agrad_i, dw_i, small_i,
+    upd_h, agrad_h, lw_h, lb_h, rw_h, rb_h, dw_h, ob_h, gain_h, shift_h,
+    upd_v, agrad_v, dw_v, small_v, dw_f, lw_f, rw_f, lb_f, rb_f, ob_f, gain_f, shift_f, sem,
+):
+    copies = []
+
+    def send(src, dst):
+        copies.append(pltpu.make_async_copy(src, dst, sem.at[len(copies)]))
+        copies[-1].start()
+
+    fetches = [
+        pltpu.make_async_copy(src, dst, sem.at[10 + n])
+        for n, (src, dst) in enumerate(((dw_i, dw_v), (small_i, small_v), (upd_i, upd_v), (agrad_i, agrad_v)))
+    ]
+    for f in fetches:
+        f.start()
+    fetches[0].wait()
+    for d in range(NDP):
+        for a in range(4):
+            dw_f[:, d * 4 + a, :] = dw_v[d, a * 32:(a + 1) * 32, :].astype(F32)
+    send(dw_f, dw_h)
+    fetches[2].wait()
+    send(upd_v, upd_h)
+    fetches[3].wait()
+    send(agrad_v, agrad_h)
+    fetches[1].wait()
+
+    def tail(c, k):
+        return small_v[c, k].astype(F32)[8:9]
+
+    for c, (buf, out) in enumerate(((lw_f, lw_h), (rw_f, rw_h))):
+        for half in range(2):
+            rows = [small_v[c, half * 4 + d].astype(F32)[0:8] for d in range(4)]
+            buf[:, half * 128:(half + 1) * 128] = jnp.concatenate(rows, axis=0)
+        send(buf, out)
+    ob_f[...] = tail(0, 0)
+    lb_f[...] = tail(0, 1)[:, 0:C_H]
+    rb_f[...] = tail(1, 4)[:, 0:C_H]
+    gain_f[...] = jnp.concatenate([tail(1, 0), tail(1, 1)], axis=1)
+    shift_f[...] = jnp.concatenate([tail(1, 2), tail(1, 3)], axis=1)
+    for buf, out in ((ob_f, ob_h), (lb_f, lb_h), (rb_f, rb_h), (gain_f, gain_h), (shift_f, shift_h)):
+        send(buf, out)
+    for c in copies:
+        c.wait()
 
 
 def body(
     alignment, chain_ids, row_counts, norm_gain, norm_shift, left_weight, left_bias,
     right_weight, right_bias, out_weight, out_bias, pair_cotangent,
 ):
-    wt = jnp.concatenate([left_weight, right_weight], axis=1).T
-    bias = jnp.concatenate([left_bias, right_bias])
-    vm = pl.BlockSpec(memory_space=pltpu.VMEM)
-    sm = pl.BlockSpec(memory_space=pltpu.SMEM)
     sems = lambda *shape: pltpu.SemaphoreType.DMA(shape)
     vmem = pltpu.VMEM
     scratch = [
-        vmem((128 * ROWS, C_M), BF16), vmem((ROWS, N, C_Z), BF16),
+        vmem((ROWS, N, C_Z), BF16), vmem((128 * ROWS, C_M), BF16), pltpu.SMEM((1, N), jnp.int32), pltpu.SMEM((1, CHAINS), jnp.int32), vmem((1, N), jnp.int32),
+        vmem((128 * ROWS, C_M), BF16), vmem((1, C_M), F32), vmem((1, C_M), F32), vmem((1, C_H), F32),
+        vmem((1, C_H), F32), vmem((C_H * C_H, C_Z), BF16), vmem((1, C_Z), F32), vmem((ROWS, N, C_Z), BF16),
+        vmem((2 * C_H, C_M), BF16), vmem((C_H * C_H, C_Z), F32), vmem((C_H, C_H * C_Z), BF16),
         vmem((ENT, C_M), F32), vmem((ENT, C_M), BF16), vmem((ENT, 1), F32),
         vmem((ENT, C_H), BF16), vmem((C_H, ENT), BF16), vmem((256, 128), BF16),
         vmem((2048, 1024), BF16), vmem((512, 1024), BF16), vmem((N, 1024), BF16), vmem((N, 1024), BF16),
@@ -561,45 +616,58 @@
         vmem((NZ, 16, C_Z), BF16), vmem((NDP, 128, C_Z), BF16),
         vmem((2, NDP, 16, C_Z), BF16), vmem((2, NDP, 16, C_Z), BF16), vmem((2, NRES, 16, C_Z), BF16), vmem((2, NDP, 16, C_Z), BF16),
         vmem((ENT, C_M), BF16),
-        sems(2), sems(NZ), sems(NZ), sems(2, NZ), sems(2, NZ), sems(2, NZ), sems(2, NZ),
+        sems(13), sems(5), sems(NZ), sems(NZ), sems(2, NZ), sems(2, NZ), sems(2, NZ), sems(2, NZ),
         sems(2, NZ), sems(2, NZ), sems(2, NZ), sems(2, NZ), sems(NZ), sems(NZ),
         sems(NDP), sems(NDP), sems(NZ), sems(NZ), sems(NY), sems(NY), sems(NZ), sems(NZ), sems(NDP), sems(NDP),
-        sems(2, NDP), sems(2, NDP), sems(2, NRES), sems(2, NRES), sems(2, NDP), sems(2, NDP),
+        sems(2, NDP), sems(2, NDP), sems(2), sems(2), sems(2, NDP), sems(2, NDP),
     ]
-    hbm = pl.BlockSpec(memory_space=pl.ANY)
-    upd, agrad, dw, lw, rw, tails = pl.pallas_call(
+    hbm = pl.BlockSpec(memory_space=pltpu.HBM)
+    upd, agrad, dw, small = pl.pallas_call(
         kernel,
         out_shape=(
             jax.ShapeDtypeStruct((ROWS, N, C_Z), BF16),
             jax.ShapeDtypeStruct((128 * ROWS, C_M), BF16),
-            jax.ShapeDtypeStruct((C_H, C_H, C_Z), F32),
-            jax.ShapeDtypeStruct((C_M, C_H), F32),
-            jax.ShapeDtypeStruct((C_M, C_H), F32),
-            jax.ShapeDtypeStruct((16, C_Z), F32),
+            jax.ShapeDtypeStruct((NDP, 128, C_Z), BF16),
+            jax.ShapeDtypeStruct((2, NDP, 16, C_Z), BF16),
         ),
-        in_specs=[sm, sm, vm, hbm] + [vm] * 7 + [hbm],
-        out_specs=(vm,) * 6,
+        in_specs=[hbm] * 12,
+        out_specs=(hbm,) * 4,
         scratch_shapes=scratch,
         compiler_params=pltpu.CompilerParams(
-            collective_id=0, has_side_effects=True, vmem_limit_bytes=50 * 1024 * 1024
+            collective_id=0, has_side_effects=True, vmem_limit_bytes=56 * 1024 * 1024
         ),
     )(
-        chain_ids, row_counts, chain_ids, alignment.reshape(128 * ROWS, C_M),
-        norm_gain.reshape(1, C_M), norm_shift.reshape(1, C_M), wt,
-        bias.reshape(2, C_H), bias.reshape(2 * C_H, 1),
-        out_weight.reshape(C_H, C_H * C_Z), out_bias.reshape(1, C_Z), pair_cotangent[0],
+        chain_ids, row_counts, alignment.reshape(128 * ROWS, C_M),
+        norm_gain.reshape(1, C_M), norm_shift.reshape(1, C_M), left_weight.T, left_bias.reshape(1, C_H),
+        right_weight.T, right_bias.reshape(1, C_H), out_weight, out_bias.reshape(1, C_Z), pair_cotangent[0],
     )
+    outs = (
+        ((ROWS, N, C_Z), BF16), ((128 * ROWS, C_M), BF16), ((C_H, C_M), F32), ((1, C_H), F32), ((C_H, C_M), F32),
+        ((1, C_H), F32), ((C_H, C_H, C_Z), F32), ((1, C_Z), F32), ((1, C_M), F32), ((1, C_M), F32),
+    )
+    upd, agrad, lw, lb, rw, rb, dw, ob, gain, shift = pl.pallas_call(
+        finish,
+        out_shape=tuple(jax.ShapeDtypeStruct(*o) for o in outs),
+        in_specs=[hbm] * 4,
+        out_specs=(hbm,) * 10,
+        scratch_shapes=[
+            vmem((ROWS, N, C_Z), BF16), vmem((128 * ROWS, C_M), BF16),
+            vmem((NDP, 128, C_Z), BF16), vmem((2, NDP, 16, C_Z), BF16), vmem((C_H, C_H, C_Z), F32), vmem((C_H, C_M), F32), vmem((C_H, C_M), F32), vmem((1, C_H), F32), vmem((1, C_H), F32),
+            vmem((1, C_Z), F32), vmem((1, C_M), F32), vmem((1, C_M), F32), sems(14),
+        ],
+        compiler_params=pltpu.CompilerParams(vmem_limit_bytes=56 * 1024 * 1024),
+    )(upd, agrad, dw, small)
     return (
         upd[None],
         agrad.reshape(1, 128, ROWS, C_M),
-        lw,
-        tails[1, 0:C_H],
-        rw,
-        tails[12, 0:C_H],
+        lw.T,
+        lb.reshape(C_H),
+        rw.T,
+        rb.reshape(C_H),
         dw.reshape(C_H * C_H, C_Z),
-        tails[0],
-        tails[8:10].reshape(C_M),
-        tails[10:12].reshape(C_M),
+        ob.reshape(C_Z),
+        gain.reshape(C_M),
+        shift.reshape(C_M),
     )
 
 

time: 79 us -> 70.5 us (0.89)
  local copies, waits for them, and re-layouts: 9.06 us -> 0 us
  Pallas kernels: 68.8 us -> 69.7 us
    unnamed x27 -> x0, local copies, waits for them, and re-layouts: 6.15 us -> none
    pallas_call x0 -> x1, Pallas kernels: none -> 2.71 us  [body(): pl.pallas_call(finish, out_shape=tuple((jax.ShapeDtypeStruct(*o) for o in...]
    reshape x4 -> x0, local copies, waits for them, and re-layouts: 1.87 us -> none  [the longest x1 1.12 us: body(): out_weight.reshape(C_H, C_H * C_Z)]
    pallas_call x1, Pallas kernels: 68.8 us -> 67 us  [body(): pl.pallas_call(kernel, out_shape=(jax.ShapeDtypeStruct((ROWS, N, C_Z), BF...]
    squeeze x2 -> x0, local copies, waits for them, and re-layouts: 1.03 us -> none  [the longest x1 0.52 us: body(): tails[12, 0:C_H]]
where the time goes in v3:
time: 70.5 us; the launch traced here: 70.4 us
  Pallas kernels  69.7 us (99%)
    pallas_call x1, Pallas kernels, body(): pl.pallas_call(kernel, out_shape=(jax.ShapeDtypeStruct((ROWS, N, C_Z), BF...  67 us
    pallas_call x1, Pallas kernels, body(): pl.pallas_call(finish, out_shape=tuple((jax.ShapeDtypeStruct(*o) for o in...  2.71 us

profile of v3, /device:TPU:1, one launch (start us, length us, event | category | flops | bytes accessed | tf_op | source)
XLA Modules:
  0.0 70.4 jit_solution(4069425899530604187)
XLA Ops:
  0.6 67.0 %shard_map.195 = (bf16[8,256,128]{2,1,0:T(8,128)(2,1)}, bf16[1024,256]{1,0:T(8,128)(2,1)}, bf16[8,128,128]{2,1,0:T(8,128)(2,1)}, bf16[2,8,16,128]{3,2,1,0:T(8,128)(2,1)}) custom-call(s32[1,256]{1,0:T(1,128)} %chain_h.1, s32[1,12]{1,0:T(1,128)} %counts_h.1, bf16[1024,256]{1,0:T(8,128)(2,1)} %bitcast.19, f32[1,256]{1,0:T(1,128)} %bitcast.23, ...), custom_call_target="tpu_custom_call" | custom-call | tf_op jit(solution)/shard_map/pallas_call | solution.py:625
  67.7 2.7 %shard_map.196 = (bf16[8,256,128]{2,1,0:T(8,128)(2,1)}, bf16[1024,256]{1,0:T(8,128)(2,1)}, f32[32,256]{1,0:T(8,128)}, f32[1,32]{1,0:T(1,128)}, f32[32,256]{1,0:T...) custom-call(bf16[8,256,128]{2,1,0:T(8,128)(2,1)} %get-tuple-element., ...), custom_call_target="tpu_custom_call" | custom-call | tf_op jit(solution)/shard_map/pallas_call | solution.py:648

commit v4 on v3

--- a/solution.py
+++ b/solution.py
@@ -50,11 +50,11 @@
     upd_ref, agrad_ref, chain_s, counts_s, chain_v, x_ref, gain_ref, shift_ref, lb_ref, rb_ref, w_ref, obias_ref, cot_ref,
     wt_ref, wf, w2_ref,
     xc, normed, inv_ref, lrow, lt, q_ref, tp, tu, g_ref, gm_ref, v_ref, rx, rp, ru,
-    ry1, ry2, vsum, rz, ucat, dwf, dws, a_rx, s1, b_rx, c_rx, s4, d_rx,
-    sm, t_rx, e_rx, so, ract,
+    ry1, ry2, vsum, rz, ucat, dwf, dws, a_rx, c_rx, d_rx,
+    sm, t_rx, e_rx, f_rx, so, ract,
     in_s, out_s, agz_s, agz_r, agy_s, agy_r, agf_s, agf_r, rs1_s, rs1_r, rs2_s, rs2_r, rsz_s, rsz_r,
-    p_s, p_r, bz_s, bz_r, cy_s, cy_r, dz_s, dz_r, ed_s, ed_r,
-    td_s, td_r, ur_s, ur_r, wd_s, wd_r,
+    p_s, p_r, cz_s, cz_r, ed_s, ed_r,
+    td_s, td_r, uy_s, uy_r, uz_s, uz_r, wd_s, wd_r,
 ):
     me = lax.axis_index("res")
     dp = lax.axis_index("dp")
@@ -92,8 +92,18 @@
     def _(k):
         pl.semaphore_signal(barrier, inc=1, device_id={"res": (me + k) % NRES}, device_id_type=MESH)
 
-    for k in range(1, NDP):
-        pl.semaphore_signal(barrier, inc=1, device_id={"dp": dpeer(k)}, device_id_type=MESH)
+    owner = dp * NY + y
+
+    def opeer(k):
+        o = (owner + k) % C_H
+        return {"dp": o // NY, "res": z * NY + o % NY}
+
+    @pl.loop(1, NDP)
+    def _(k):
+        for j in range(NY):
+            pl.semaphore_signal(
+                barrier, inc=1, device_id={"dp": dpeer(k), "res": z * NY + ypeer(j)}, device_id_type=MESH
+            )
 
     for f in fetches[:10]:
         f.wait()
@@ -160,7 +170,7 @@
             [mixed[(8 * q + a) * 16:(8 * q + a + 1) * 16, PAIRED:SLOTS] for a in range(8)], axis=1
         ).astype(BF16)
 
-    pl.semaphore_wait(barrier, NRES + NDP - 2)
+    pl.semaphore_wait(barrier, NRES - 1 + NY * (NDP - 1))
 
     def agz(k):
         return rc(rx.at[me], rx.at[me], agz_s.at[k], agz_r.at[k], res=zpeer(k) * NY + y)
@@ -209,12 +219,9 @@
                 tp[pl.ds(rowp + a * 64, 64), i * 128:(i + 1) * 128] = t[i * SLOTS:i * SLOTS + PAIRED, a * 128:(a + 1) * 128]
                 tu[pl.ds(rowu + a * 16, 16), i * 128:(i + 1) * 128] = t[i * SLOTS + PAIRED:(i + 1) * SLOTS, a * 128:(a + 1) * 128]
 
-    pl.loop(0, 12)(t_step)
+    pl.loop(0, 12, unroll=2)(t_step)
     spread(1, 7)
-    pl.loop(12, 16)(t_step)
-    spread(2, 6)
-    forward(0)
-
+    pl.loop(12, 16, unroll=2)(t_step)
     chain_col = jnp.transpose(jnp.broadcast_to(chain_v[...].astype(F32), (128, N)))
     obg = jnp.zeros((8, C_Z), F32)
     inv_own = []
@@ -228,9 +235,6 @@
         g_ref[:, i * 128:(i + 1) * 128] = g
         gm_ref[:, i * 128:(i + 1) * 128] = jnp.where(same, g.astype(F32), 0.0).astype(BF16)
 
-    spread(3, 5)
-    forward(1, 7)
-
     def put_v(v, lane):
         both = jnp.concatenate(
             [v[:, 0:128].reshape(NRES, ROWS, 128), v[:, 128:256].reshape(NRES, ROWS, 128)], axis=1
@@ -272,21 +276,28 @@
                 rsz(kz).start()
         return total
 
-    pl.loop(0, 4)(v_step)
+    def first(*turns):
+        for kz in turns:
+            for d in range(2):
+                rs1(d, kz).start()
+
+    pl.loop(0, 4, unroll=2)(v_step)
+    spread(2, 6)
+    forward(0)
+    pl.loop(4, 8, unroll=2)(v_step)
+    for q in range(2):
+        put_v(dot(gm_ref[...], tu[q * 256:(q + 1) * 256, :], NT), 1024 + q * 128)
+    first(4, 3, 5, 2)
+    spread(3, 5)
+    forward(1, 7)
+    first(6, 1, 7, 0)
     spread(4)
     forward(2, 6)
-    pl.loop(4, 8)(v_step)
-    forward(3)
-    for q in range(2):
-        put_v(dot(gm_ref[...], tu[q * 256:(q + 1) * 256, :], NT), 1024 + q * 128)
-    forward(5)
-    for kz in (4, 3, 5, 2, 6):
-        for d in range(2):
-            rs1(d, kz).start()
+    second(4)
+    forward(3, 5)
+    second(3, 5)
     forward(4)
-    for kz in (1, 7, 0):
-        for d in range(2):
-            rs1(d, kz).start()
+    second(2, 6)
 
     for kz in range(NZ):
         for d in range(2):
@@ -311,12 +322,7 @@
                 for i in range(ROWS):
                     ucat[i * SLOTS:i * SLOTS + PAIRED, pl.ds(lane, 128)] = u[(h * 2 + a) * 64:(h * 2 + a + 1) * 64, i * 128:(i + 1) * 128]
 
-    pl.loop(0, 3)(u_step)
-    second(4, 3, 5)
-    pl.loop(3, 6)(u_step)
-    second(2, 6, 1)
-    pl.loop(6, 8)(u_step)
-    for q in range(2):
+    def u_side(q):
         u = dot(ru[:, q * 256:(q + 1) * 256], gm_ref[...], TN).astype(BF16)
         for h in range(2):
             for a in range(8):
@@ -324,71 +330,75 @@
                 for i in range(ROWS):
                     ucat[i * SLOTS + PAIRED:(i + 1) * SLOTS, lane:lane + 128] = u[(h * 8 + a) * 16:(h * 8 + a + 1) * 16, i * 128:(i + 1) * 128]
 
-    second(7, 0)
-    third(4, 3, 5)
-
-    @pl.loop(0, 16)
-    def _(g):
-        dw = dot(lt[...], ucat[:, pl.ds(pl.multiple_of(g * 256, 256), 256)])
+    def pd(e):
+        k = (e - owner + C_H) % C_H
+        return rc(dws.at[e], a_rx.at[k - 1], p_s.at[0], p_r.at[0], **opeer(k))
+
+    def dw_step(g):
+        dw = dot(lt[...], ucat[:, g * 256:(g + 1) * 256])
         for a in range(2):
             part = dw[:, a * 128:(a + 1) * 128]
-            row = pl.multiple_of((g % 2) * 64 + a * 32, 32)
-            dwf[g // 2, pl.ds(row, 32), :] = part
-            dws[g // 2, pl.ds(row, 32), :] = part.astype(BF16)
-
-    def pdp(k):
-        return rc(dws.at[dpeer(k)], a_rx.at[k], p_s.at[k], p_r.at[k], dp=dpeer(k))
-
-    for k in range(1, NDP):
-        pdp(k).start()
-
-    own = third(2, 6, 1, 7, 0)
+            dwf[2 * g + a] = part
+            dws[2 * g + a] = part.astype(BF16)
+
+    def dw_send(first):
+        @pl.loop(first, first + 8)
+        def _(e):
+            @pl.when(e != owner)
+            def _():
+                pd(e).start()
+
+    pl.loop(0, 4, unroll=2)(u_step)
+    u_side(0)
+    second(1, 7, 0)
+    for g in (0, 1, 2, 3, 8, 9, 10, 11):
+        dw_step(g)
+    dw_send(0)
+    dw_send(16)
+    third(4, 3, 5)
+    pl.loop(4, 8, unroll=2)(u_step)
+    u_side(1)
+    third(2, 6)
+    for g in (4, 5, 6, 7, 12, 13, 14, 15):
+        dw_step(g)
+    dw_send(8)
+    dw_send(24)
+    own = third(1, 7, 0)
 
     def left_step(k, acc):
         cols = pl.ds(pl.multiple_of(k * 512, 512), 512)
         return acc + dot(ucat[:, cols], w2_ref[:, cols], NT)
 
-    lgrad = lax.fori_loop(0, 8, left_step, jnp.zeros((ENT, C_H), F32))
-
-    def td(c, k):
-        return rc(sm.at[c, dpeer(k)], t_rx.at[c, k], td_s.at[c, k], td_r.at[c, k], dp=dpeer(k))
-
-    def ur(c, k):
-        return rc(e_rx.at[c, me], e_rx.at[c, me], ur_s.at[c], ur_r.at[c], res=(me + k) % NRES)
-
-    def wd(c, k):
-        return rc(so.at[c, dp], so.at[c, dp], wd_s.at[c, k], wd_r.at[c, k], dp=dpeer(k))
+    lgrad = lax.fori_loop(0, 8, left_step, jnp.zeros((ENT, C_H), F32), unroll=2)
+
+    def td(k):
+        return rc(sm.at[dpeer(k)], t_rx.at[k - 1], td_s.at[0], td_r.at[0], dp=dpeer(k))
+
+    def uy(k):
+        return rc(e_rx.at[y], e_rx.at[y], uy_s.at[0], uy_r.at[0], res=z * NY + ypeer(k))
+
+    def uz(k):
+        return rc(f_rx.at[z], f_rx.at[z], uz_s.at[0], uz_r.at[0], res=zpeer(k) * NY + y)
+
+    def wd(k):
+        return rc(so.at[dp], so.at[dp], wd_s.at[0], wd_r.at[0], dp=dpeer(k))
 
     rows8 = iota((8, C_Z), 0)
 
-    def small_first(c, gw, tail_rows):
+    def small_put(c, gw, tail_rows):
         tail = jnp.zeros((8, C_Z), F32)
         for k, row in enumerate(tail_rows):
             tail = jnp.where(rows8 == k, row, tail)
         main = jnp.concatenate([gw[:, 0:128], gw[:, 128:256]], axis=0).reshape(8, 8, C_Z)
         tails = jnp.broadcast_to(tail.reshape(8, 1, C_Z), (8, 8, C_Z))
-        sm[c] = jnp.concatenate([main, tails], axis=1).astype(BF16)
-        for k in range(1, NDP):
-            td(c, k).start()
-
-    def small_second(c):
-        s = sm[c, dp].astype(F32)
-        for k in range(1, NDP):
-            td(c, k).wait_recv()
-            s = s + t_rx[c, k].astype(F32)
-        e_rx[c, me] = s.astype(BF16)
-
-        @pl.loop(1, NRES)
-        def _(k):
-            ur(c, k).start()
-
-    def small_third(c):
-        others = e_rx.at[c, 0:NRES - 1]
-        rc(others, others, ur_s.at[c], ur_r.at[c], res=(me + 1) % NRES).wait()
-
-        so[c, dp] = (jnp.sum(e_rx[c].astype(F32), axis=0) * (1.0 / N)).astype(BF16)
-        for k in range(1, NDP):
-            wd(c, k).start()
+        sm[:, c * 16:(c + 1) * 16, :] = jnp.concatenate([main, tails], axis=1).astype(BF16)
+
+    def drain(ref, send, recv, count):
+        some = ref.at[0:count]
+        rc(some, some, send.at[0], recv.at[0], dp=dpeer(1)).wait()
+
+    def total(ref):
+        return jnp.sum(ref[...].astype(F32), axis=0)
 
     gw_l = jnp.zeros((C_H, C_M), F32)
     gb_l = jnp.zeros((1, C_H), F32)
@@ -398,24 +408,10 @@
         gw_l = gw_l + dot(lact, normed[rows, :], TN)
         gb_l = gb_l + jnp.sum(lact.astype(F32), axis=0, keepdims=True)
         lrow[rows, :] = lact
-    small_first(0, gw_l, (
+    small_put(0, gw_l, (
         jnp.sum(obg, axis=0, keepdims=True),
         jnp.concatenate([gb_l, jnp.zeros((1, 96), F32)], axis=1),
     ))
-
-    s = dwf[dp]
-    for k in range(1, NDP):
-        pdp(k).wait_recv()
-        s = s + a_rx[k].astype(F32)
-    s1[...] = s.reshape(NZ, 16, C_Z)
-
-    def bz(k):
-        return rc(s1.at[zpeer(k)], b_rx.at[k], bz_s.at[k], bz_r.at[k], res=zpeer(k) * NY + y)
-
-    for k in range(1, NZ):
-        bz(k).start()
-
-    small_second(0)
 
     for kz in (4, 3, 5, 2, 6, 1, 7):
         rsz(kz).wait_recv()
@@ -443,36 +439,46 @@
         mean_p = jnp.mean(gg * scaled, axis=-1, keepdims=True)
         ract[rows, :] = (inv_ref[rows, :] * (gg - mean_g - scaled * mean_p)).astype(BF16)
     gbr_row = jnp.transpose(jnp.broadcast_to(gb_r, (C_H, 128)))[0:1, :]
-    small_first(1, gw_r, (
+    small_put(1, gw_r, (
         gain_g[:, 0:128], gain_g[:, 128:256], shift_g[:, 0:128], shift_g[:, 128:256],
         jnp.concatenate([gbr_row, jnp.zeros((1, 96), F32)], axis=1),
     ))
 
-    s = s1[z]
+    for k in range(1, NDP):
+        td(k).start()
+
+    drain(a_rx, p_s, p_r, C_H - 1)
+
+    def add(k, t):
+        return t + a_rx[k].astype(F32)
+
+    c_rx[z] = lax.fori_loop(0, C_H - 1, add, dwf[owner], unroll=True).astype(BF16)
+
+    def cz(k):
+        return rc(c_rx.at[z], c_rx.at[z], cz_s.at[0], cz_r.at[0], res=zpeer(k) * NY + y)
+
     for k in range(1, NZ):
-        bz(k).wait_recv()
-        s = s + b_rx[k]
-    c_rx[y] = s
-
-    def cy(k):
-        return rc(c_rx.at[y], c_rx.at[y], cy_s.at[k], cy_r.at[k], res=z * NY + ypeer(k))
-
+        cz(k).start()
+
+    drain(t_rx, td_s, td_r, NDP - 1)
+    e_rx[y] = (sm[dp].astype(F32) + total(t_rx)).astype(BF16)
     for k in range(1, NY):
-        cy(k).start()
-
-    small_second(1)
-
-    for k in range(1, NY):
-        cy(k).wait_recv()
-    s4[z] = ((c_rx[0] + c_rx[1] + c_rx[2] + c_rx[3]) * (1.0 / N)).astype(BF16)
-
-    def dz(k):
-        return rc(s4.at[z], s4.at[z], dz_s.at[k], dz_r.at[k], res=zpeer(k) * NY + y)
-
+        uy(k).start()
+
+    drain(c_rx, cz_s, cz_r, NZ - 1)
+    d_rx[owner] = (total(c_rx) * (1.0 / N)).astype(BF16)
+
+    def ed(k):
+        return rc(d_rx.at[owner], d_rx.at[owner], ed_s.at[0], ed_r.at[0], **opeer(k))
+
+    @pl.loop(1, C_H)
+    def _(k):
+        ed(k).start()
+
+    drain(e_rx, uy_s, uy_r, NY - 1)
+    f_rx[z] = total(e_rx).astype(BF16)
     for k in range(1, NZ):
-        dz(k).start()
-
-    small_third(0)
+        uz(k).start()
 
     @pl.loop(0, 4)
     def _(g):
@@ -500,50 +506,29 @@
     upd_out = pltpu.make_async_copy(upd_ref, upd_h, out_s.at[0])
     upd_out.start()
 
-    for k in range(1, NZ):
-        dz(k).wait_recv()
-    d_rx[dp] = s4[...].reshape(128, C_Z)
-
-    def ed(k):
-        return rc(d_rx.at[dp], d_rx.at[dp], ed_s.at[k], ed_r.at[k], dp=dpeer(k))
-
-    for k in range(1, NDP):
-        ed(k).start()
-
-    small_third(1)
     agrad_out = pltpu.make_async_copy(agrad_ref, agrad_h, out_s.at[1])
     agrad_out.start()
+
+    drain(f_rx, uz_s, uz_r, NZ - 1)
+    so[dp] = (total(f_rx) * (1.0 / N)).astype(BF16)
+    for k in range(1, NDP):
+        wd(k).start()
+
     for kz in range(NZ):
         for d in range(2):
             for c in (agy, agf, rs1, rs2):
                 c(d, kz).wait_send()
     for k in range(1, NZ):
-        for c in (agz, rsz, bz, dz):
-            c(k).wait_send()
-    for k in range(1, NDP):
-        pdp(k).wait_send()
-        td(0, k).wait_send()
-        td(1, k).wait_send()
-        wd(0, k).wait_send()
-    for k in range(1, NY):
-        cy(k).wait_send()
-
-    for k in range(1, NDP):
-        wd(0, k).wait_recv()
-    small0_out = pltpu.make_async_copy(so.at[0], small_h.at[0], out_s.at[2])
-    small0_out.start()
-    for k in range(1, NDP):
-        ed(k).wait_recv()
-    dw_out = pltpu.make_async_copy(d_rx, dw_h, out_s.at[3])
+        agz(k).wait_send()
+        rsz(k).wait_send()
+
+    drain(d_rx, ed_s, ed_r, C_H - 1)
+    dw_out = pltpu.make_async_copy(d_rx, dw_h, out_s.at[2])
     dw_out.start()
-    for k in range(1, NDP):
-        wd(1, k).wait_recv()
-    small1_out = pltpu.make_async_copy(so.at[1], small_h.at[1], out_s.at[4])
-    small1_out.start()
-    for k in range(1, NDP):
-        ed(k).wait_send()
-        wd(1, k).wait_send()
-    for c in (upd_out, agrad_out, small0_out, dw_out, small1_out):
+    drain(so, wd_s, wd_r, NDP - 1)
+    small_out = pltpu.make_async_copy(so, small_h, out_s.at[3])
+    small_out.start()
+    for c in (upd_out, agrad_out, dw_out, small_out):
         c.wait()
 
 
@@ -567,7 +552,7 @@
     fetches[0].wait()
     for d in range(NDP):
         for a in range(4):
-            dw_f[:, d * 4 + a, :] = dw_v[d, a * 32:(a + 1) * 32, :].astype(F32)
+            dw_f[:, d * 4 + a, :] = dw_v[d * 4 + a].astype(F32)
     send(dw_f, dw_h)
     fetches[2].wait()
     send(upd_v, upd_h)
@@ -576,11 +561,11 @@
     fetches[1].wait()
 
     def tail(c, k):
-        return small_v[c, k].astype(F32)[8:9]
+        return small_v[k].astype(F32)[c * 16 + 8:c * 16 + 9]
 
     for c, (buf, out) in enumerate(((lw_f, lw_h), (rw_f, rw_h))):
         for half in range(2):
-            rows = [small_v[c, half * 4 + d].astype(F32)[0:8] for d in range(4)]
+            rows = [small_v[half * 4 + d].astype(F32)[c * 16:c * 16 + 8] for d in range(4)]
             buf[:, half * 128:(half + 1) * 128] = jnp.concatenate(rows, axis=0)
         send(buf, out)
     ob_f[...] = tail(0, 0)
@@ -611,15 +596,14 @@
         vmem((NRES, 16, 1280), BF16), vmem((NRES, 16, 1280), BF16), vmem((N, 2048), BF16), vmem((N, 512), BF16),
         vmem((2, NZ, 16, HALF), BF16), vmem((2, NZ, 16, 1280), BF16), vmem((NZ, 16, 1280), BF16), vmem((NZ, 16, 1280), BF16),
         vmem((ENT, 4096), BF16),
-        vmem((NDP, 128, C_Z), F32), vmem((NDP, 128, C_Z), BF16), vmem((NDP, 128, C_Z), BF16),
-        vmem((NZ, 16, C_Z), F32), vmem((NZ, 16, C_Z), F32), vmem((NY, 16, C_Z), F32),
-        vmem((NZ, 16, C_Z), BF16), vmem((NDP, 128, C_Z), BF16),
-        vmem((2, NDP, 16, C_Z), BF16), vmem((2, NDP, 16, C_Z), BF16), vmem((2, NRES, 16, C_Z), BF16), vmem((2, NDP, 16, C_Z), BF16),
+        vmem((C_H, C_H, C_Z), F32), vmem((C_H, C_H, C_Z), BF16), vmem((C_H - 1, C_H, C_Z), BF16),
+        vmem((NZ, C_H, C_Z), BF16), vmem((C_H, C_H, C_Z), BF16),
+        vmem((NDP, 32, C_Z), BF16), vmem((NDP - 1, 32, C_Z), BF16), vmem((NY, 32, C_Z), BF16), vmem((NZ, 32, C_Z), BF16), vmem((NDP, 32, C_Z), BF16),
         vmem((ENT, C_M), BF16),
-        sems(13), sems(5), sems(NZ), sems(NZ), sems(2, NZ), sems(2, NZ), sems(2, NZ), sems(2, NZ),
+        sems(13), sems(4), sems(NZ), sems(NZ), sems(2, NZ), sems(2, NZ), sems(2, NZ), sems(2, NZ),
         sems(2, NZ), sems(2, NZ), sems(2, NZ), sems(2, NZ), sems(NZ), sems(NZ),
-        sems(NDP), sems(NDP), sems(NZ), sems(NZ), sems(NY), sems(NY), sems(NZ), sems(NZ), sems(NDP), sems(NDP),
-        sems(2, NDP), sems(2, NDP), sems(2), sems(2), sems(2, NDP), sems(2, NDP),
+        sems(1), sems(1), sems(1), sems(1), sems(1), sems(1),
+        sems(1), sems(1), sems(1), sems(1), sems(1), sems(1), sems(1), sems(1),
     ]
     hbm = pl.BlockSpec(memory_space=pltpu.HBM)
     upd, agrad, dw, small = pl.pallas_call(
@@ -627,8 +611,8 @@
         out_shape=(
             jax.ShapeDtypeStruct((ROWS, N, C_Z), BF16),
             jax.ShapeDtypeStruct((128 * ROWS, C_M), BF16),
-            jax.ShapeDtypeStruct((NDP, 128, C_Z), BF16),
-            jax.ShapeDtypeStruct((2, NDP, 16, C_Z), BF16),
+            jax.ShapeDtypeStruct((C_H, C_H, C_Z), BF16),
+            jax.ShapeDtypeStruct((NDP, 32, C_Z), BF16),
         ),
         in_specs=[hbm] * 12,
         out_specs=(hbm,) * 4,
@@ -652,7 +636,7 @@
         out_specs=(hbm,) * 10,
         scratch_shapes=[
             vmem((ROWS, N, C_Z), BF16), vmem((128 * ROWS, C_M), BF16),
-            vmem((NDP, 128, C_Z), BF16), vmem((2, NDP, 16, C_Z), BF16), vmem((C_H, C_H, C_Z), F32), vmem((C_H, C_M), F32), vmem((C_H, C_M), F32), vmem((1, C_H), F32), vmem((1, C_H), F32),
+            vmem((C_H, C_H, C_Z), BF16), vmem((NDP, 32, C_Z), BF16), vmem((C_H, C_H, C_Z), F32), vmem((C_H, C_M), F32), vmem((C_H, C_M), F32), vmem((1, C_H), F32), vmem((1, C_H), F32),
             vmem((1, C_Z), F32), vmem((1, C_M), F32), vmem((1, C_M), F32), sems(14),
         ],
         compiler_params=pltpu.CompilerParams(vmem_limit_bytes=56 * 1024 * 1024),

time: 70.5 us -> 67.3 us (0.955)
  Pallas kernels: 69.7 us -> 66.5 us
    pallas_call x1, Pallas kernels: 67 us -> 63.8 us  [body(): pl.pallas_call(kernel, out_shape=(jax.ShapeDtypeStruct((ROWS, N, C_Z), BF...]
where the time goes in v4:
time: 67.3 us; the launch traced here: 67.1 us
  Pallas kernels  66.5 us (99%)
    pallas_call x1, Pallas kernels, body(): pl.pallas_call(kernel, out_shape=(jax.ShapeDtypeStruct((ROWS, N, C_Z), BF...  63.8 us
    pallas_call x1, Pallas kernels, body(): pl.pallas_call(finish, out_shape=tuple((jax.ShapeDtypeStruct(*o) for o in...  2.71 us

profile of v4, /device:TPU:1, one launch (start us, length us, event | category | flops | bytes accessed | tf_op | source)
XLA Modules:
  0.0 67.1 jit_solution(15366791965212634768)
XLA Ops:
  0.6 63.8 %shard_map.195 = (bf16[8,256,128]{2,1,0:T(8,128)(2,1)}, bf16[1024,256]{1,0:T(8,128)(2,1)}, bf16[32,32,128]{2,1,0:T(8,128)(2,1)}, bf16[8,32,128]{2,1,0:T(8,128)(2,1)}) custom-call(s32[1,256]{1,0:T(1,128)} %chain_h.1, s32[1,12]{1,0:T(1,128)} %counts_h.1, bf16[1024,256]{1,0:T(8,128)(2,1)} %bitcast.19, f32[1,256]{1,0:T(1,128)} %bitcast.23, f32[1,256]{1,0:T(1,128)} %bitcast.24, ...), custom_call_target="tpu_custom_call" | custom-call | tf_op jit(solution)/shard_map/pallas_call | solution.py:609
  64.4 2.7 %shard_map.196 = (bf16[8,256,128]{2,1,0:T(8,128)(2,1)}, bf16[1024,256]{1,0:T(8,128)(2,1)}, f32[32,256]{1,0:T(8,128)}, f32[1,32]{1,0:T(1,128)}, f32[32,256]{1,0:T...) custom-call(bf16[8,256,128]{2,1,0:T(8,128)(2,1)} %get-tuple-element., ...), custom_call_target="tpu_custom_call" | custom-call | tf_op jit(solution)/shard_map/pallas_call | solution.py:632

commit v5 on v4

--- a/solution.py
+++ b/solution.py
@@ -23,7 +23,8 @@
 NRES = NY * NZ
 N = ROWS * NRES
 ENT = ROWS * SLOTS
-HALF = 640
+MAIN = 1024
+HALF = MAIN // 2
 F32, BF16 = jnp.float32, jnp.bfloat16
 MESH = pl.DeviceIdType.MESH
 
@@ -50,9 +51,9 @@
     upd_ref, agrad_ref, chain_s, counts_s, chain_v, x_ref, gain_ref, shift_ref, lb_ref, rb_ref, w_ref, obias_ref, cot_ref,
     wt_ref, wf, w2_ref,
     xc, normed, inv_ref, lrow, lt, q_ref, tp, tu, g_ref, gm_ref, v_ref, rx, rp, ru,
-    ry1, ry2, vsum, rz, ucat, dwf, dws, a_rx, c_rx, d_rx,
+    ry1, ry2, vsum, rz, rbz, sbf, sb, rby, ucat, dwf, dws, a_rx, c_rx, d_rx,
     sm, t_rx, e_rx, f_rx, so, ract,
-    in_s, out_s, agz_s, agz_r, agy_s, agy_r, agf_s, agf_r, rs1_s, rs1_r, rs2_s, rs2_r, rsz_s, rsz_r,
+    in_s, out_s, bgy_s, bgy_r, bgz_s, bgz_r, bsz_s, bsz_r, bsy_s, bsy_r, agz_s, agz_r, agy_s, agy_r, agf_s, agf_r, rs1_s, rs1_r, rs2_s, rs2_r, rsz_s, rsz_r,
     p_s, p_r, cz_s, cz_r, ed_s, ed_r,
     td_s, td_r, uy_s, uy_r, uz_s, uz_r, wd_s, wd_r,
 ):
@@ -173,16 +174,30 @@
     pl.semaphore_wait(barrier, NRES - 1 + NY * (NDP - 1))
 
     def agz(k):
-        return rc(rx.at[me], rx.at[me], agz_s.at[k], agz_r.at[k], res=zpeer(k) * NY + y)
+        part = rx.at[me, :, 0:MAIN]
+        return rc(part, part, agz_s.at[0], agz_r.at[k], res=zpeer(k) * NY + y)
 
     def agy(d, kz):
         slot = ((z - kz + NZ) % NZ) * NY + y
-        return rc(rx.at[slot], rx.at[slot], agy_s.at[d, kz], agy_r.at[d, kz], res=z * NY + ypeer(1 + 2 * d))
+        part = rx.at[slot, :, 0:MAIN]
+        return rc(part, part, agy_s.at[0], agy_r.at[d, kz], res=z * NY + ypeer(1 + 2 * d))
 
     def agf(d, kz):
         slot = ((z - kz + NZ) % NZ) * NY + ypeer(3 - 2 * d)
         part = rx.at[slot, :, d * HALF:(d + 1) * HALF]
-        return rc(part, part, agf_s.at[d, kz], agf_r.at[d, kz], res=z * NY + ypeer(1 + 2 * d))
+        return rc(part, part, agf_s.at[0], agf_r.at[0], res=z * NY + ypeer(1 + 2 * d))
+
+    def bgy(k):
+        part = rx.at[me, :, MAIN:]
+        return rc(part, part, bgy_s.at[0], bgy_r.at[0], res=z * NY + ypeer(k))
+
+    def bgz(k):
+        part = rx.at[pl.ds(z * NY, NY), :, MAIN:]
+        return rc(part, part, bgz_s.at[0], bgz_r.at[0], res=zpeer(k) * NY + y)
+
+    def drain(ref, send, recv, count):
+        some = ref.at[0:count]
+        rc(some, some, send.at[0], recv.at[0], dp=dpeer(1)).wait()
 
     def spread(*turns):
         for kz in turns:
@@ -197,9 +212,11 @@
                 agy(d, kz).wait_recv()
                 agf(d, kz).start()
 
-    spread(0)
+    for k in range(1, NY):
+        bgy(k).start()
     for k in (1, 7, 2, 6, 3, 5, 4):
         agz(k).start()
+    spread(0)
 
     for f in fetches[10:]:
         f.wait()
@@ -222,6 +239,11 @@
     pl.loop(0, 12, unroll=2)(t_step)
     spread(1, 7)
     pl.loop(12, 16, unroll=2)(t_step)
+    spread(2, 6)
+    drain(rx.at[:, :, MAIN:], bgy_s, bgy_r, NY - 1)
+    for k in range(1, NZ):
+        bgz(k).start()
+    forward(0)
     chain_col = jnp.transpose(jnp.broadcast_to(chain_v[...].astype(F32), (128, N)))
     obg = jnp.zeros((8, C_Z), F32)
     inv_own = []
@@ -235,6 +257,9 @@
         g_ref[:, i * 128:(i + 1) * 128] = g
         gm_ref[:, i * 128:(i + 1) * 128] = jnp.where(same, g.astype(F32), 0.0).astype(BF16)
 
+    spread(3, 5)
+    forward(1, 7)
+
     def put_v(v, lane):
         both = jnp.concatenate(
             [v[:, 0:128].reshape(NRES, ROWS, 128), v[:, 128:256].reshape(NRES, ROWS, 128)], axis=1
@@ -247,14 +272,28 @@
     def rs1(d, kz):
         dst = zpeer(kz) * NY + ypeer(2)
         src = v_ref.at[dst, :, d * HALF:(d + 1) * HALF]
-        return rc(src, ry1.at[d, kz], rs1_s.at[d, kz], rs1_r.at[d, kz], res=z * NY + ypeer(3 - 2 * d))
+        return rc(src, ry1.at[d, kz], rs1_s.at[0], rs1_r.at[d, kz], res=z * NY + ypeer(3 - 2 * d))
 
     def rs2(d, kz):
         dst = zpeer(kz) * NY + ypeer(3 - 2 * d)
-        return rc(v_ref.at[dst], ry2.at[d, kz], rs2_s.at[d, kz], rs2_r.at[d, kz], res=z * NY + ypeer(3 - 2 * d))
+        return rc(v_ref.at[dst, :, 0:MAIN], ry2.at[d, kz], rs2_s.at[0], rs2_r.at[d, kz], res=z * NY + ypeer(3 - 2 * d))
 
     def rsz(k):
-        return rc(vsum.at[k], rz.at[k], rsz_s.at[k], rsz_r.at[k], res=zpeer(k) * NY + y)
+        return rc(vsum.at[k - 1], rz.at[k - 1], rsz_s.at[0], rsz_r.at[0], res=zpeer(k) * NY + y)
+
+    def bsz(k):
+        src = v_ref.at[pl.ds(zpeer(k) * NY, NY), :, MAIN:]
+        return rc(src, rbz.at[k - 1], bsz_s.at[0], bsz_r.at[0], res=zpeer(k) * NY + y)
+
+    def bsy(k):
+        return rc(sb.at[ypeer(k)], rby.at[k - 1], bsy_s.at[0], bsy_r.at[0], res=z * NY + ypeer(k))
+
+    def side_sums():
+        drain(rbz, bsz_s, bsz_r, NZ - 1)
+        sbf[...] = v_ref[pl.ds(z * NY, NY), :, MAIN:].astype(F32) + jnp.sum(rbz[...].astype(F32), axis=0)
+        sb[...] = sbf[...].astype(BF16)
+        for k in range(1, NY):
+            bsy(k).start()
 
     def second(*turns):
         for kz in turns:
@@ -267,12 +306,12 @@
 
     def third(*turns):
         for kz in turns:
-            total = v_ref[zpeer(kz) * NY + y].astype(F32)
+            total = v_ref[zpeer(kz) * NY + y, :, 0:MAIN].astype(F32)
             for d in range(2):
                 rs2(d, kz).wait_recv()
                 total = total + ry2[d, kz].astype(F32)
             if kz:
-                vsum[kz] = total.astype(BF16)
+                vsum[kz - 1] = total.astype(BF16)
                 rsz(kz).start()
         return total
 
@@ -281,27 +320,22 @@
             for d in range(2):
                 rs1(d, kz).start()
 
+    for q in range(2):
+        put_v(dot(gm_ref[...], tu[q * 256:(q + 1) * 256, :], NT), MAIN + q * 128)
     pl.loop(0, 4, unroll=2)(v_step)
-    spread(2, 6)
-    forward(0)
+    spread(4)
+    for k in range(1, NZ):
+        bsz(k).start()
+    forward(2, 6)
     pl.loop(4, 8, unroll=2)(v_step)
-    for q in range(2):
-        put_v(dot(gm_ref[...], tu[q * 256:(q + 1) * 256, :], NT), 1024 + q * 128)
-    first(4, 3, 5, 2)
-    spread(3, 5)
-    forward(1, 7)
-    first(6, 1, 7, 0)
-    spread(4)
-    forward(2, 6)
-    second(4)
-    forward(3, 5)
-    second(3, 5)
+    forward(3)
+    forward(5)
+    first(4, 3, 5, 2, 6)
     forward(4)
-    second(2, 6)
-
-    for kz in range(NZ):
-        for d in range(2):
-            agf(d, kz).wait_recv()
+    first(1, 7, 0)
+    drain(rx.at[:, :, 0:HALF], agf_s, agf_r, 2 * NZ)
+    second(4, 3, 5, 2, 6, 1, 7, 0)
+    drain(rx.at[:, :, MAIN:], bgz_s, bgz_r, NY * (NZ - 1))
 
     @pl.loop(0, NRES // 2)
     def _(d):
@@ -350,20 +384,19 @@
 
     pl.loop(0, 4, unroll=2)(u_step)
     u_side(0)
-    second(1, 7, 0)
     for g in (0, 1, 2, 3, 8, 9, 10, 11):
         dw_step(g)
     dw_send(0)
     dw_send(16)
+    pl.loop(4, 8, unroll=2)(u_step)
     third(4, 3, 5)
-    pl.loop(4, 8, unroll=2)(u_step)
+    side_sums()
     u_side(1)
-    third(2, 6)
     for g in (4, 5, 6, 7, 12, 13, 14, 15):
         dw_step(g)
     dw_send(8)
     dw_send(24)
-    own = third(1, 7, 0)
+    own = third(2, 6, 1, 7, 0)
 
     def left_step(k, acc):
         cols = pl.ds(pl.multiple_of(k * 512, 512), 512)
@@ -392,10 +425,6 @@
         main = jnp.concatenate([gw[:, 0:128], gw[:, 128:256]], axis=0).reshape(8, 8, C_Z)
         tails = jnp.broadcast_to(tail.reshape(8, 1, C_Z), (8, 8, C_Z))
         sm[:, c * 16:(c + 1) * 16, :] = jnp.concatenate([main, tails], axis=1).astype(BF16)
-
-    def drain(ref, send, recv, count):
-        some = ref.at[0:count]
-        rc(some, some, send.at[0], recv.at[0], dp=dpeer(1)).wait()
 
     def total(ref):
         return jnp.sum(ref[...].astype(F32), axis=0)
@@ -413,9 +442,11 @@
         jnp.concatenate([gb_l, jnp.zeros((1, 96), F32)], axis=1),
     ))
 
-    for kz in (4, 3, 5, 2, 6, 1, 7):
-        rsz(kz).wait_recv()
-        own = own + rz[kz].astype(F32)
+    drain(rz, rsz_s, rsz_r, NZ - 1)
+    drain(rby, bsy_s, bsy_r, NY - 1)
+    own = jnp.concatenate(
+        [own + jnp.sum(rz[...].astype(F32), axis=0), sbf[y] + jnp.sum(rby[...].astype(F32), axis=0)], axis=1
+    )
     tiles = []
     for e in range(16):
         tiles.append(jnp.concatenate([own[:, e * 64:(e + 1) * 64], own[:, 1024 + e * 16:1024 + (e + 1) * 16]], axis=1))
@@ -514,13 +545,13 @@
     for k in range(1, NDP):
         wd(k).start()
 
-    for kz in range(NZ):
-        for d in range(2):
-            for c in (agy, agf, rs1, rs2):
-                c(d, kz).wait_send()
-    for k in range(1, NZ):
-        agz(k).wait_send()
-        rsz(k).wait_send()
+    def sent(ref, sem):
+        rc(ref, ref, sem.at[0], sem.at[0], dp=dpeer(1)).wait_send()
+
+    sent(rx.at[0:NZ - 1, :, 0:MAIN], agz_s)
+    sent(rx.at[0:2 * NZ, :, 0:MAIN], agy_s)
+    sent(v_ref.at[0:2 * NZ, :, 0:HALF], rs1_s)
+    sent(v_ref.at[0:2 * NZ, :, 0:MAIN], rs2_s)
 
     drain(d_rx, ed_s, ed_r, C_H - 1)
     dw_out = pltpu.make_async_copy(d_rx, dw_h, out_s.at[2])
@@ -594,14 +625,16 @@
         vmem((ENT, C_H), BF16), vmem((C_H, ENT), BF16), vmem((256, 128), BF16),
         vmem((2048, 1024), BF16), vmem((512, 1024), BF16), vmem((N, 1024), BF16), vmem((N, 1024), BF16),
         vmem((NRES, 16, 1280), BF16), vmem((NRES, 16, 1280), BF16), vmem((N, 2048), BF16), vmem((N, 512), BF16),
-        vmem((2, NZ, 16, HALF), BF16), vmem((2, NZ, 16, 1280), BF16), vmem((NZ, 16, 1280), BF16), vmem((NZ, 16, 1280), BF16),
+        vmem((2, NZ, 16, HALF), BF16), vmem((2, NZ, 16, MAIN), BF16), vmem((NZ - 1, 16, MAIN), BF16), vmem((NZ - 1, 16, MAIN), BF16),
+        vmem((NZ - 1, NY, 16, 256), BF16), vmem((NY, 16, 256), F32), vmem((NY, 16, 256), BF16), vmem((NY - 1, 16, 256), BF16),
         vmem((ENT, 4096), BF16),
         vmem((C_H, C_H, C_Z), F32), vmem((C_H, C_H, C_Z), BF16), vmem((C_H - 1, C_H, C_Z), BF16),
         vmem((NZ, C_H, C_Z), BF16), vmem((C_H, C_H, C_Z), BF16),
         vmem((NDP, 32, C_Z), BF16), vmem((NDP - 1, 32, C_Z), BF16), vmem((NY, 32, C_Z), BF16), vmem((NZ, 32, C_Z), BF16), vmem((NDP, 32, C_Z), BF16),
         vmem((ENT, C_M), BF16),
-        sems(13), sems(4), sems(NZ), sems(NZ), sems(2, NZ), sems(2, NZ), sems(2, NZ), sems(2, NZ),
-        sems(2, NZ), sems(2, NZ), sems(2, NZ), sems(2, NZ), sems(NZ), sems(NZ),
+        sems(13), sems(4), sems(1), sems(1), sems(1), sems(1), sems(1), sems(1), sems(1), sems(1),
+        sems(1), sems(NZ), sems(1), sems(2, NZ), sems(1), sems(1),
+        sems(1), sems(2, NZ), sems(1), sems(2, NZ), sems(1), sems(1),
         sems(1), sems(1), sems(1), sems(1), sems(1), sems(1),
         sems(1), sems(1), sems(1), sems(1), sems(1), sems(1), sems(1), sems(1),
     ]

time: 67.3 us -> 62.8 us (0.933)
  Pallas kernels: 66.5 us -> 62 us
    pallas_call x1, Pallas kernels: 63.8 us -> 59.3 us  [body(): pl.pallas_call(kernel, out_shape=(jax.ShapeDtypeStruct((ROWS, N, C_Z), BF...]
where the time goes in v5:
time: 62.8 us; the launch traced here: 62.6 us
  Pallas kernels  62 us (99%)
  between operations  0.66 us (1%)
    pallas_call x1, Pallas kernels, body(): pl.pallas_call(kernel, out_shape=(jax.ShapeDtypeStruct((ROWS, N, C_Z), BF...  59.3 us
    pallas_call x1, Pallas kernels, body(): pl.pallas_call(finish, out_shape=tuple((jax.ShapeDtypeStruct(*o) for o in...  2.71 us

profile of v5, /device:TPU:1, one launch (start us, length us, event | category | flops | bytes accessed | tf_op | source)
XLA Modules:
  0.0 62.6 jit_solution(14650554914059309037)
XLA Ops:
  0.6 59.3 %shard_map.195 = (bf16[8,256,128]{2,1,0:T(8,128)(2,1)}, bf16[1024,256]{1,0:T(8,128)(2,1)}, bf16[32,32,128]{2,1,0:T(8,128)(2,1)}, bf16[8,32,128]{2,1,0:T(8,128)(2,1)}) custom-call(s32[1,256]{1,0:T(1,128)} %chain_h.1, s32[1,12]{1,0:T(1,128)} %counts_h.1, bf16[1024,256]{1,0:T(8,128)(2,1)} %bitcast.19, f32[1,256]{1,0:T(1,128)} %bitcast.23, f32[1,256]{1,0:T(1,128)} %bitcast.24, ...), custom_call_target="tpu_custom_call" | custom-call | tf_op jit(solution)/shard_map/pallas_call | solution.py:642
  59.9 2.7 %shard_map.196 = (bf16[8,256,128]{2,1,0:T(8,128)(2,1)}, bf16[1024,256]{1,0:T(8,128)(2,1)}, f32[32,256]{1,0:T(8,128)}, f32[1,32]{1,0:T(1,128)}, f32[32,256]{1,0:T...) custom-call(bf16[8,256,128]{2,1,0:T(8,128)(2,1)} %get-tuple-element., ...), custom_call_target="tpu_custom_call" | custom-call | tf_op jit(solution)/shard_map/pallas_call | solution.py:665

commit v6 on v5

--- a/solution.py
+++ b/solution.py
@@ -52,10 +52,10 @@
     wt_ref, wf, w2_ref,
     xc, normed, inv_ref, lrow, lt, q_ref, tp, tu, g_ref, gm_ref, v_ref, rx, rp, ru,
     ry1, ry2, vsum, rz, rbz, sbf, sb, rby, ucat, dwf, dws, a_rx, c_rx, d_rx,
-    sm, t_rx, e_rx, f_rx, so, ract,
+    sm, t_rx, f_rx, so, ract,
     in_s, out_s, bgy_s, bgy_r, bgz_s, bgz_r, bsz_s, bsz_r, bsy_s, bsy_r, agz_s, agz_r, agy_s, agy_r, agf_s, agf_r, rs1_s, rs1_r, rs2_s, rs2_r, rsz_s, rsz_r,
     p_s, p_r, cz_s, cz_r, ed_s, ed_r,
-    td_s, td_r, uy_s, uy_r, uz_s, uz_r, wd_s, wd_r,
+    td_s, td_r, uz_s, uz_r, wd_s, wd_r,
 ):
     me = lax.axis_index("res")
     dp = lax.axis_index("dp")
@@ -240,9 +240,6 @@
     spread(1, 7)
     pl.loop(12, 16, unroll=2)(t_step)
     spread(2, 6)
-    drain(rx.at[:, :, MAIN:], bgy_s, bgy_r, NY - 1)
-    for k in range(1, NZ):
-        bgz(k).start()
     forward(0)
     chain_col = jnp.transpose(jnp.broadcast_to(chain_v[...].astype(F32), (128, N)))
     obg = jnp.zeros((8, C_Z), F32)
@@ -258,6 +255,9 @@
         gm_ref[:, i * 128:(i + 1) * 128] = jnp.where(same, g.astype(F32), 0.0).astype(BF16)
 
     spread(3, 5)
+    drain(rx.at[:, :, MAIN:], bgy_s, bgy_r, NY - 1)
+    for k in range(1, NZ):
+        bgz(k).start()
     forward(1, 7)
 
     def put_v(v, lane):
@@ -302,6 +302,10 @@
                 lanes = slice(d * HALF, (d + 1) * HALF)
                 rs1(d, kz).wait_recv()
                 v_ref[slab, :, lanes] = (v_ref[slab, :, lanes].astype(F32) + ry1[d, kz].astype(F32)).astype(BF16)
+
+    def pass_on(*turns):
+        for kz in turns:
+            for d in range(2):
                 rs2(d, kz).start()
 
     def third(*turns):
@@ -324,8 +328,6 @@
         put_v(dot(gm_ref[...], tu[q * 256:(q + 1) * 256, :], NT), MAIN + q * 128)
     pl.loop(0, 4, unroll=2)(v_step)
     spread(4)
-    for k in range(1, NZ):
-        bsz(k).start()
     forward(2, 6)
     pl.loop(4, 8, unroll=2)(v_step)
     forward(3)
@@ -333,8 +335,13 @@
     first(4, 3, 5, 2, 6)
     forward(4)
     first(1, 7, 0)
+    for k in range(1, NZ):
+        bsz(k).start()
+    second(4, 3, 5, 2)
+    pass_on(4, 3, 5, 2)
+    second(6, 1, 7, 0)
     drain(rx.at[:, :, 0:HALF], agf_s, agf_r, 2 * NZ)
-    second(4, 3, 5, 2, 6, 1, 7, 0)
+    pass_on(6, 1, 7, 0)
     drain(rx.at[:, :, MAIN:], bgz_s, bgz_r, NY * (NZ - 1))
 
     @pl.loop(0, NRES // 2)
@@ -389,14 +396,15 @@
     dw_send(0)
     dw_send(16)
     pl.loop(4, 8, unroll=2)(u_step)
+    u_side(1)
     third(4, 3, 5)
     side_sums()
-    u_side(1)
+    third(2)
     for g in (4, 5, 6, 7, 12, 13, 14, 15):
         dw_step(g)
     dw_send(8)
     dw_send(24)
-    own = third(2, 6, 1, 7, 0)
+    own = third(6, 1, 7, 0)
 
     def left_step(k, acc):
         cols = pl.ds(pl.multiple_of(k * 512, 512), 512)
@@ -405,10 +413,8 @@
     lgrad = lax.fori_loop(0, 8, left_step, jnp.zeros((ENT, C_H), F32), unroll=2)
 
     def td(k):
-        return rc(sm.at[dpeer(k)], t_rx.at[k - 1], td_s.at[0], td_r.at[0], dp=dpeer(k))
-
-    def uy(k):
-        return rc(e_rx.at[y], e_rx.at[y], uy_s.at[0], uy_r.at[0], res=z * NY + ypeer(k))
+        slot = (owner + k) % C_H // NY
+        return rc(sm.at[slot], t_rx.at[owner], td_s.at[0], td_r.at[0], **opeer(k))
 
     def uz(k):
         return rc(f_rx.at[z], f_rx.at[z], uz_s.at[0], uz_r.at[0], res=zpeer(k) * NY + y)
@@ -475,7 +481,8 @@
         jnp.concatenate([gbr_row, jnp.zeros((1, 96), F32)], axis=1),
     ))
 
-    for k in range(1, NDP):
+    @pl.loop(1, C_H)
+    def _(k):
         td(k).start()
 
     drain(a_rx, p_s, p_r, C_H - 1)
@@ -491,10 +498,11 @@
     for k in range(1, NZ):
         cz(k).start()
 
-    drain(t_rx, td_s, td_r, NDP - 1)
-    e_rx[y] = (sm[dp].astype(F32) + total(t_rx)).astype(BF16)
-    for k in range(1, NY):
-        uy(k).start()
+    t_rx[owner] = sm[dp]
+    drain(t_rx, td_s, td_r, C_H - 1)
+    f_rx[z] = total(t_rx).astype(BF16)
+    for k in range(1, NZ):
+        uz(k).start()
 
     drain(c_rx, cz_s, cz_r, NZ - 1)
     d_rx[owner] = (total(c_rx) * (1.0 / N)).astype(BF16)
@@ -505,11 +513,6 @@
     @pl.loop(1, C_H)
     def _(k):
         ed(k).start()
-
-    drain(e_rx, uy_s, uy_r, NY - 1)
-    f_rx[z] = total(e_rx).astype(BF16)
-    for k in range(1, NZ):
-        uz(k).start()
 
     @pl.loop(0, 4)
     def _(g):
@@ -630,13 +633,13 @@
         vmem((ENT, 4096), BF16),
         vmem((C_H, C_H, C_Z), F32), vmem((C_H, C_H, C_Z), BF16), vmem((C_H - 1, C_H, C_Z), BF16),
         vmem((NZ, C_H, C_Z), BF16), vmem((C_H, C_H, C_Z), BF16),
-        vmem((NDP, 32, C_Z), BF16), vmem((NDP - 1, 32, C_Z), BF16), vmem((NY, 32, C_Z), BF16), vmem((NZ, 32, C_Z), BF16), vmem((NDP, 32, C_Z), BF16),
+        vmem((NDP, 32, C_Z), BF16), vmem((C_H, 32, C_Z), BF16), vmem((NZ, 32, C_Z), BF16), vmem((NDP, 32, C_Z), BF16),
         vmem((ENT, C_M), BF16),
         sems(13), sems(4), sems(1), sems(1), sems(1), sems(1), sems(1), sems(1), sems(1), sems(1),
         sems(1), sems(NZ), sems(1), sems(2, NZ), sems(1), sems(1),
         sems(1), sems(2, NZ), sems(1), sems(2, NZ), sems(1), sems(1),
         sems(1), sems(1), sems(1), sems(1), sems(1), sems(1),
-        sems(1), sems(1), sems(1), sems(1), sems(1), sems(1), sems(1), sems(1),
+        sems(1), sems(1), sems(1), sems(1), sems(1), sems(1),
     ]
     hbm = pl.BlockSpec(memory_space=pltpu.HBM)
     upd, agrad, dw, small = pl.pallas_call(

time: 62.8 us -> 60.3 us (0.960)
  Pallas kernels: 62 us -> 59.5 us
    pallas_call x1, Pallas kernels: 59.3 us -> 56.8 us  [body(): pl.pallas_call(kernel, out_shape=(jax.ShapeDtypeStruct((ROWS, N, C_Z), BF...]
where the time goes in v6:
time: 60.3 us; the launch traced here: 60.2 us
  Pallas kernels  59.5 us (99%)
  between operations  0.66 us (1%)
    pallas_call x1, Pallas kernels, body(): pl.pallas_call(kernel, out_shape=(jax.ShapeDtypeStruct((ROWS, N, C_Z), BF...  56.8 us
    pallas_call x1, Pallas kernels, body(): pl.pallas_call(finish, out_shape=tuple((jax.ShapeDtypeStruct(*o) for o in...  2.71 us

profile of v6, /device:TPU:1, one launch (start us, length us, event | category | flops | bytes accessed | tf_op | source)
XLA Modules:
  0.0 60.2 jit_solution(9003512007768729648)
XLA Ops:
  0.6 56.8 %shard_map.195 = (bf16[8,256,128]{2,1,0:T(8,128)(2,1)}, bf16[1024,256]{1,0:T(8,128)(2,1)}, bf16[32,32,128]{2,1,0:T(8,128)(2,1)}, bf16[8,32,128]{2,1,0:T(8,128)(2,1)}) custom-call(s32[1,256]{1,0:T(1,128)} %chain_h.1, s32[1,12]{1,0:T(1,128)} %counts_h.1, bf16[1024,256]{1,0:T(8,128)(2,1)} %bitcast.19, f32[1,256]{1,0:T(1,128)} %bitcast.23, f32[1,256]{1,0:T(1,128)} %bitcast.24, ...), custom_call_target="tpu_custom_call" | custom-call | tf_op jit(solution)/shard_map/pallas_call | solution.py:645
  57.5 2.7 %shard_map.196 = (bf16[8,256,128]{2,1,0:T(8,128)(2,1)}, bf16[1024,256]{1,0:T(8,128)(2,1)}, f32[32,256]{1,0:T(8,128)}, f32[1,32]{1,0:T(1,128)}, f32[32,256]{1,0:T...) custom-call(bf16[8,256,128]{2,1,0:T(8,128)(2,1)} %get-tuple-element., ...), custom_call_target="tpu_custom_call" | custom-call | tf_op jit(solution)/shard_map/pallas_call | solution.py:668

commit v7 on v6

--- a/solution.py
+++ b/solution.py
@@ -52,7 +52,7 @@
     wt_ref, wf, w2_ref,
     xc, normed, inv_ref, lrow, lt, q_ref, tp, tu, g_ref, gm_ref, v_ref, rx, rp, ru,
     ry1, ry2, vsum, rz, rbz, sbf, sb, rby, ucat, dwf, dws, a_rx, c_rx, d_rx,
-    sm, t_rx, f_rx, so, ract,
+    sm, t_rx, f_rx, so, ract, gn_ref,
     in_s, out_s, bgy_s, bgy_r, bgz_s, bgz_r, bsz_s, bsz_r, bsy_s, bsy_r, agz_s, agz_r, agy_s, agy_r, agf_s, agf_r, rs1_s, rs1_r, rs2_s, rs2_r, rsz_s, rsz_r,
     p_s, p_r, cz_s, cz_r, ed_s, ed_r,
     td_s, td_r, uz_s, uz_r, wd_s, wd_r,
@@ -339,9 +339,11 @@
         bsz(k).start()
     second(4, 3, 5, 2)
     pass_on(4, 3, 5, 2)
-    second(6, 1, 7, 0)
+    second(6)
+    pass_on(6)
+    second(1, 7, 0)
     drain(rx.at[:, :, 0:HALF], agf_s, agf_r, 2 * NZ)
-    pass_on(6, 1, 7, 0)
+    pass_on(1, 7, 0)
     drain(rx.at[:, :, MAIN:], bgz_s, bgz_r, NY * (NZ - 1))
 
     @pl.loop(0, NRES // 2)
@@ -395,11 +397,11 @@
         dw_step(g)
     dw_send(0)
     dw_send(16)
+    third(4, 3)
     pl.loop(4, 8, unroll=2)(u_step)
     u_side(1)
-    third(4, 3, 5)
+    third(5, 2)
     side_sums()
-    third(2)
     for g in (4, 5, 6, 7, 12, 13, 14, 15):
         dw_step(g)
     dw_send(8)
@@ -442,7 +444,7 @@
         lact = (lgrad[rows] * slot_mask(r, (SLOTS, C_H), 0)).astype(BF16)
         gw_l = gw_l + dot(lact, normed[rows, :], TN)
         gb_l = gb_l + jnp.sum(lact.astype(F32), axis=0, keepdims=True)
-        lrow[rows, :] = lact
+        gn_ref[rows, :] = dot(lact, wt_ref[0:C_H, :])
     small_put(0, gw_l, (
         jnp.sum(obg, axis=0, keepdims=True),
         jnp.concatenate([gb_l, jnp.zeros((1, 96), F32)], axis=1),
@@ -467,14 +469,10 @@
         ract_t = (back[r * C_H:(r + 1) * C_H, :] * slot_mask(r, (C_H, SLOTS), 1)).astype(BF16)
         gw_r = gw_r + dot(ract_t, normed[rows, :])
         gb_r = gb_r + jnp.sum(ract_t.astype(F32), axis=1, keepdims=True)
-        gn = dot(lrow[rows, :], wt_ref[0:C_H, :]) + dot(ract_t, wt_ref[C_H:, :], TN)
-        scaled = xc[rows, :]
-        gain_g = gain_g + jnp.sum(gn * scaled, axis=0, keepdims=True)
+        gn = gn_ref[rows, :] + dot(ract_t, wt_ref[C_H:, :], TN)
+        gn_ref[rows, :] = gn
+        gain_g = gain_g + jnp.sum(gn * xc[rows, :], axis=0, keepdims=True)
         shift_g = shift_g + jnp.sum(gn, axis=0, keepdims=True)
-        gg = gn * gain_ref[...]
-        mean_g = jnp.mean(gg, axis=-1, keepdims=True)
-        mean_p = jnp.mean(gg * scaled, axis=-1, keepdims=True)
-        ract[rows, :] = (inv_ref[rows, :] * (gg - mean_g - scaled * mean_p)).astype(BF16)
     gbr_row = jnp.transpose(jnp.broadcast_to(gb_r, (C_H, 128)))[0:1, :]
     small_put(1, gw_r, (
         gain_g[:, 0:128], gain_g[:, 128:256], shift_g[:, 0:128], shift_g[:, 128:256],
@@ -531,6 +529,13 @@
             out = jnp.where(same, (m + s) * iv, m * (1.0 / (PAIRED + NORM_FLOOR))) + obias_ref[...]
             upd_ref[i] = out.astype(BF16)
 
+    for r in range(ROWS):
+        rows = slice(r * SLOTS, (r + 1) * SLOTS)
+        scaled = xc[rows, :]
+        gg = gn_ref[rows, :] * gain_ref[...]
+        mean_g = jnp.mean(gg, axis=-1, keepdims=True)
+        mean_p = jnp.mean(gg * scaled, axis=-1, keepdims=True)
+        ract[rows, :] = (inv_ref[rows, :] * (gg - mean_g - scaled * mean_p)).astype(BF16)
     for b in range(PAIRED // 16):
         src = jnp.concatenate([ract[r * SLOTS + b * 16:r * SLOTS + b * 16 + 16, :] for r in range(ROWS)], axis=0)
         agrad_ref[b * 128:(b + 1) * 128, :] = dot(perm0, src, TN).astype(BF16)
@@ -634,7 +639,7 @@
         vmem((C_H, C_H, C_Z), F32), vmem((C_H, C_H, C_Z), BF16), vmem((C_H - 1, C_H, C_Z), BF16),
         vmem((NZ, C_H, C_Z), BF16), vmem((C_H, C_H, C_Z), BF16),
         vmem((NDP, 32, C_Z), BF16), vmem((C_H, 32, C_Z), BF16), vmem((NZ, 32, C_Z), BF16), vmem((NDP, 32, C_Z), BF16),
-        vmem((ENT, C_M), BF16),
+        vmem((ENT, C_M), BF16), vmem((ENT, C_M), F32),
         sems(13), sems(4), sems(1), sems(1), sems(1), sems(1), sems(1), sems(1), sems(1), sems(1),
         sems(1), sems(NZ), sems(1), sems(2, NZ), sems(1), sems(1),
         sems(1), sems(2, NZ), sems(1), sems(2, NZ), sems(1), sems(1),

time: 60.3 us -> 59.4 us (0.985)
  Pallas kernels: 59.5 us -> 58.6 us
    pallas_call x1, Pallas kernels: 56.8 us -> 55.9 us  [body(): pl.pallas_call(kernel, out_shape=(jax.ShapeDtypeStruct((ROWS, N, C_Z), BF...]
where the time goes in v7:
time: 59.4 us; the launch traced here: 59.3 us
  Pallas kernels  58.6 us (99%)
  between operations  0.66 us (1%)
    pallas_call x1, Pallas kernels, body(): pl.pallas_call(kernel, out_shape=(jax.ShapeDtypeStruct((ROWS, N, C_Z), BF...  55.9 us
    pallas_call x1, Pallas kernels, body(): pl.pallas_call(finish, out_shape=tuple((jax.ShapeDtypeStruct(*o) for o in...  2.71 us

profile of v7, /device:TPU:1, one launch (start us, length us, event | category | flops | bytes accessed | tf_op | source)
XLA Modules:
  0.0 59.3 jit_solution(15582721843327332325)
XLA Ops:
  0.6 55.9 %shard_map.195 = (bf16[8,256,128]{2,1,0:T(8,128)(2,1)}, bf16[1024,256]{1,0:T(8,128)(2,1)}, bf16[32,32,128]{2,1,0:T(8,128)(2,1)}, bf16[8,32,128]{2,1,0:T(8,128)(2,1)}) custom-call(s32[1,256]{1,0:T(1,128)} %chain_h.1, s32[1,12]{1,0:T(1,128)} %counts_h.1, bf16[1024,256]{1,0:T(8,128)(2,1)} %bitcast.19, f32[1,256]{1,0:T(1,128)} %bitcast.23, f32[1,256]{1,0:T(1,128)} %bitcast.24, ...), custom_call_target="tpu_custom_call" | custom-call | tf_op jit(solution)/shard_map/pallas_call | solution.py:650
  56.6 2.7 %shard_map.196 = (bf16[8,256,128]{2,1,0:T(8,128)(2,1)}, bf16[1024,256]{1,0:T(8,128)(2,1)}, f32[32,256]{1,0:T(8,128)}, f32[1,32]{1,0:T(1,128)}, f32[32,256]{1,0:T...) custom-call(bf16[8,256,128]{2,1,0:T(8,128)(2,1)} %get-tuple-element., ...), custom_call_target="tpu_custom_call" | custom-call | tf_op jit(solution)/shard_map/pallas_call | solution.py:673

commit v8 on v7

--- a/solution.py
+++ b/solution.py
@@ -395,18 +395,18 @@
     u_side(0)
     for g in (0, 1, 2, 3, 8, 9, 10, 11):
         dw_step(g)
+    third(4, 3)
     dw_send(0)
     dw_send(16)
-    third(4, 3)
     pl.loop(4, 8, unroll=2)(u_step)
     u_side(1)
     third(5, 2)
     side_sums()
     for g in (4, 5, 6, 7, 12, 13, 14, 15):
         dw_step(g)
+    own = third(6, 1, 7, 0)
     dw_send(8)
     dw_send(24)
-    own = third(6, 1, 7, 0)
 
     def left_step(k, acc):
         cols = pl.ds(pl.multiple_of(k * 512, 512), 512)
@@ -529,6 +529,14 @@
             out = jnp.where(same, (m + s) * iv, m * (1.0 / (PAIRED + NORM_FLOOR))) + obias_ref[...]
             upd_ref[i] = out.astype(BF16)
 
+    upd_out = pltpu.make_async_copy(upd_ref, upd_h, out_s.at[0])
+    upd_out.start()
+
+    drain(f_rx, uz_s, uz_r, NZ - 1)
+    so[dp] = (total(f_rx) * (1.0 / N)).astype(BF16)
+    for k in range(1, NDP):
+        wd(k).start()
+
     for r in range(ROWS):
         rows = slice(r * SLOTS, (r + 1) * SLOTS)
         scaled = xc[rows, :]
@@ -542,16 +550,8 @@
     src = jnp.concatenate([ract[r * SLOTS + PAIRED:(r + 1) * SLOTS, :] for r in range(ROWS)], axis=0)
     agrad_ref[PAIRED * ROWS:, :] = dot(pick, src, TN).astype(BF16)
 
-    upd_out = pltpu.make_async_copy(upd_ref, upd_h, out_s.at[0])
-    upd_out.start()
-
     agrad_out = pltpu.make_async_copy(agrad_ref, agrad_h, out_s.at[1])
     agrad_out.start()
-
-    drain(f_rx, uz_s, uz_r, NZ - 1)
-    so[dp] = (total(f_rx) * (1.0 / N)).astype(BF16)
-    for k in range(1, NDP):
-        wd(k).start()
 
     def sent(ref, sem):
         rc(ref, ref, sem.at[0], sem.at[0], dp=dpeer(1)).wait_send()
@@ -583,20 +583,21 @@
         copies[-1].start()
 
     fetches = [
-        pltpu.make_async_copy(src, dst, sem.at[10 + n])
+        pltpu.make_async_copy(src, dst, sem.at[11 + n])
         for n, (src, dst) in enumerate(((dw_i, dw_v), (small_i, small_v), (upd_i, upd_v), (agrad_i, agrad_v)))
     ]
     for f in fetches:
         f.start()
-    fetches[0].wait()
-    for d in range(NDP):
-        for a in range(4):
-            dw_f[:, d * 4 + a, :] = dw_v[d * 4 + a].astype(F32)
-    send(dw_f, dw_h)
     fetches[2].wait()
     send(upd_v, upd_h)
     fetches[3].wait()
     send(agrad_v, agrad_h)
+    fetches[0].wait()
+    for half in range(2):
+        rows = slice(half * 16, (half + 1) * 16)
+        for e in range(C_H):
+            dw_f[rows, e, :] = dw_v[e, rows, :].astype(F32)
+        send(dw_f.at[rows], dw_h.at[rows])
     fetches[1].wait()
 
     def tail(c, k):
@@ -678,7 +679,7 @@
         scratch_shapes=[
             vmem((ROWS, N, C_Z), BF16), vmem((128 * ROWS, C_M), BF16),
             vmem((C_H, C_H, C_Z), BF16), vmem((NDP, 32, C_Z), BF16), vmem((C_H, C_H, C_Z), F32), vmem((C_H, C_M), F32), vmem((C_H, C_M), F32), vmem((1, C_H), F32), vmem((1, C_H), F32),
-            vmem((1, C_Z), F32), vmem((1, C_M), F32), vmem((1, C_M), F32), sems(14),
+            vmem((1, C_Z), F32), vmem((1, C_M), F32), vmem((1, C_M), F32), sems(15),
         ],
         compiler_params=pltpu.CompilerParams(vmem_limit_bytes=56 * 1024 * 1024),
     )(upd, agrad, dw, small)

time: 59.4 us -> 59.4 us (level)
  no operation moved by 1% of the time
where the time goes in v8:
time: 59.4 us; the launch traced here: 59.3 us
  Pallas kernels  58.6 us (99%)
  between operations  0.66 us (1%)
    pallas_call x1, Pallas kernels, body(): pl.pallas_call(kernel, out_shape=(jax.ShapeDtypeStruct((ROWS, N, C_Z), BF...  56.1 us
    pallas_call x1, Pallas kernels, body(): pl.pallas_call(finish, out_shape=tuple((jax.ShapeDtypeStruct(*o) for o in...  2.57 us

profile of v8, /device:TPU:1, one launch (start us, length us, event | category | flops | bytes accessed | tf_op | source)
XLA Modules:
  0.0 59.3 jit_solution(10891796348072147945)
XLA Ops:
  0.6 56.1 %shard_map.195 = (bf16[8,256,128]{2,1,0:T(8,128)(2,1)}, bf16[1024,256]{1,0:T(8,128)(2,1)}, bf16[32,32,128]{2,1,0:T(8,128)(2,1)}, bf16[8,32,128]{2,1,0:T(8,128)(2,1)}) custom-call(s32[1,256]{1,0:T(1,128)} %chain_h.1, s32[1,12]{1,0:T(1,128)} %counts_h.1, bf16[1024,256]{1,0:T(8,128)(2,1)} %bitcast.19, f32[1,256]{1,0:T(1,128)} %bitcast.23, f32[1,256]{1,0:T(1,128)} %bitcast.24, ...), custom_call_target="tpu_custom_call" | custom-call | tf_op jit(solution)/shard_map/pallas_call | solution.py:651
  56.7 2.6 %shard_map.196 = (bf16[8,256,128]{2,1,0:T(8,128)(2,1)}, bf16[1024,256]{1,0:T(8,128)(2,1)}, f32[32,256]{1,0:T(8,128)}, f32[1,32]{1,0:T(1,128)}, f32[32,256]{1,0:T...) custom-call(bf16[8,256,128]{2,1,0:T(8,128)(2,1)} %get-tuple-element., ...), custom_call_target="tpu_custom_call" | custom-call | tf_op jit(solution)/shard_map/pallas_call | solution.py:674

commit v9 on v7

--- a/solution.py
+++ b/solution.py
@@ -89,9 +89,10 @@
 
     barrier = pltpu.get_barrier_semaphore()
 
-    @pl.loop(1, NRES)
-    def _(k):
-        pl.semaphore_signal(barrier, inc=1, device_id={"res": (me + k) % NRES}, device_id_type=MESH)
+    for k in range(1, NZ):
+        pl.semaphore_signal(barrier, inc=1, device_id={"res": zpeer(k) * NY + y}, device_id_type=MESH)
+    for k in range(1, NY):
+        pl.semaphore_signal(barrier, inc=1, device_id={"res": z * NY + ypeer(k)}, device_id_type=MESH)
 
     owner = dp * NY + y
 
@@ -171,7 +172,7 @@
             [mixed[(8 * q + a) * 16:(8 * q + a + 1) * 16, PAIRED:SLOTS] for a in range(8)], axis=1
         ).astype(BF16)
 
-    pl.semaphore_wait(barrier, NRES - 1 + NY * (NDP - 1))
+    pl.semaphore_wait(barrier, NZ + NY - 2 + NY * (NDP - 1))
 
     def agz(k):
         part = rx.at[me, :, 0:MAIN]

time: 59.4 us -> 60.1 us (1.012)
  Pallas kernels: 58.6 us -> 59.4 us
    pallas_call x1, Pallas kernels: 55.9 us -> 56.6 us  [body(): pl.pallas_call(kernel, out_shape=(jax.ShapeDtypeStruct((ROWS, N, C_Z), BF...]
where the time goes in v9:
time: 60.1 us; the launch traced here: 60 us
  Pallas kernels  59.4 us (99%)
  between operations  0.66 us (1%)
    pallas_call x1, Pallas kernels, body(): pl.pallas_call(kernel, out_shape=(jax.ShapeDtypeStruct((ROWS, N, C_Z), BF...  56.6 us
    pallas_call x1, Pallas kernels, body(): pl.pallas_call(finish, out_shape=tuple((jax.ShapeDtypeStruct(*o) for o in...  2.71 us

profile of v9, /device:TPU:1, one launch (start us, length us, event | category | flops | bytes accessed | tf_op | source)
XLA Modules:
  0.0 60.0 jit_solution(14912461070422092660)
XLA Ops:
  0.6 56.6 %shard_map.195 = (bf16[8,256,128]{2,1,0:T(8,128)(2,1)}, bf16[1024,256]{1,0:T(8,128)(2,1)}, bf16[32,32,128]{2,1,0:T(8,128)(2,1)}, bf16[8,32,128]{2,1,0:T(8,128)(2,1)}) custom-call(s32[1,256]{1,0:T(1,128)} %chain_h.1, s32[1,12]{1,0:T(1,128)} %counts_h.1, bf16[1024,256]{1,0:T(8,128)(2,1)} %bitcast.19, f32[1,256]{1,0:T(1,128)} %bitcast.23, f32[1,256]{1,0:T(1,128)} %bitcast.24, ...), custom_call_target="tpu_custom_call" | custom-call | tf_op jit(solution)/shard_map/pallas_call | solution.py:651
  57.3 2.7 %shard_map.196 = (bf16[8,256,128]{2,1,0:T(8,128)(2,1)}, bf16[1024,256]{1,0:T(8,128)(2,1)}, f32[32,256]{1,0:T(8,128)}, f32[1,32]{1,0:T(1,128)}, f32[32,256]{1,0:T...) custom-call(bf16[8,256,128]{2,1,0:T(8,128)(2,1)} %get-tuple-element., ...), custom_call_target="tpu_custom_call" | custom-call | tf_op jit(solution)/shard_map/pallas_call | solution.py:674
